TPU v7x, 32 devices: a whole 2x2x4 slice. The times are simulated.
32 devices in a mesh: tm: 2 (over core), tile: 4 (over y, x), head: 4 (over z).
Axes of the slice: x: 2, y: 2, z: 4, core: 2. Of those that a mesh axis runs over, the one named last changes fastest.
Arguments:
- query: bfloat16 [2, 4, 2, 16, 16, 1536], P('tm', 'tile', None, None, None, 'head'), may hold values from -80 to 80
- keys: bfloat16 [2, 4, 2, 16, 16, 1536], P('tm', 'tile', None, None, None, 'head'), may hold values from -80 to 80
- values: bfloat16 [2, 4, 2, 16, 16, 1536], P('tm', 'tile', None, None, None, 'head'), may hold values from -6 to 6
- out_weight: bfloat16 [1536, 1536], P('head'), may hold values from -0.15625 to 0.15625
- radius: int32 [12], P('head'), may hold values from 1 to 4
- block_mask: int32 [12, 2, 2], P('head'), may hold values from 0 to 1, as said below
Outputs:
- mixed: bfloat16 [2, 4, 512, 1536], P('tm', 'tile', 'head')
Inputs may be any that keep to these rules, and one draw needn't show every extreme that they name: For every head, block_mask is 1 on the diagonal of its table and 0 above it.
All inputs are finite; a program needn't handle non-finite values.
Results may differ from a plain program's by a relative error of at most 0.015.
Values may be sent and summed in bfloat16 or wider, within the bound.
No kernel may reach another device: no remote copies, remote signals or barrier semaphores. Data moves between devices by JAX's collectives and lax.ppermute only.
A program may use at most 128 MiB of HBM per device.

v0:
```python
import functools
import math

import jax
import jax.numpy as jnp
from jax import lax
from jax.experimental import pallas as pl
from jax.experimental.pallas import tpu as pltpu
from jax.sharding import PartitionSpec as P

RMAX = 4
FAR = -1e30
LOG2E = 1.4426950408889634
VMEM_LIMIT = 24 * 1024 * 1024


def passed_along(value, axis, by):
    peers = lax.axis_size(axis)
    pairs = [(i, i + by) for i in range(peers) if 0 <= i + by < peers]
    return lax.ppermute(value, axis, pairs)


def widen(key_part, value_part, span, row_move, col_move):
    grid = math.isqrt(lax.axis_size("tile"))
    above = None
    below = None
    for offset in (grid, -grid):
        if offset > 0:
            face_key = key_part[:, :, key_part.shape[2] - span :]
            face_value = value_part[:, :, value_part.shape[2] - span :]
        else:
            face_key = key_part[:, :, :span]
            face_value = value_part[:, :, :span]
        got = row_move(face_key, face_value, offset)
        if offset > 0:
            above = got
        else:
            below = got
    key_rows = jnp.concatenate([above[0], key_part, below[0]], axis=2)
    value_rows = jnp.concatenate([above[1], value_part, below[1]], axis=2)
    left = None
    right = None
    for offset in (1, -1):
        if offset > 0:
            face_key = key_rows[:, :, :, key_rows.shape[3] - span :]
            face_value = value_rows[:, :, :, value_rows.shape[3] - span :]
        else:
            face_key = key_rows[:, :, :, :span]
            face_value = value_rows[:, :, :, :span]
        got = col_move(face_key, face_value, offset)
        if offset > 0:
            left = got
        else:
            right = got
    key_full = jnp.concatenate([left[0], key_rows, right[0]], axis=3)
    value_full = jnp.concatenate([left[1], value_rows, right[1]], axis=3)
    return (key_full, value_full)


def windows_of(block, half_high, half_wide, win_high, win_wide, heads_here, head_dim):
    parts = []
    for band in (0, 1):
        for strip in (0, 1):
            parts.append(
                block[
                    :,
                    band * half_high : band * half_high + win_high,
                    strip * half_wide : strip * half_wide + win_wide,
                ]
            )
    stacked = jnp.stack(parts)
    return stacked.reshape(4, -1, heads_here, head_dim)


def any_grid(query, keys, values, out_weight, radius, block_mask):
    span = RMAX
    grid = math.isqrt(lax.axis_size("tile"))
    tile_at = lax.axis_index("tile")
    row_at = tile_at // grid
    col_at = tile_at % grid
    stretch_at = lax.axis_index("tm")
    frames, high, wide, channels = query.shape[2:]
    heads_here = radius.shape[0]
    head_dim = channels // heads_here
    tokens_here = frames * high * wide
    half_high = high // 2
    half_wide = wide // 2
    win_high = half_high + 2 * span
    win_wide = half_wide + 2 * span
    quarter = frames * half_high * half_wide
    queries = query[0, 0].reshape(frames, 2, half_high, 2, half_wide, channels)
    queries = queries.transpose(1, 3, 0, 2, 4, 5).reshape(4, quarter, heads_here, head_dim)
    query_y = jnp.broadcast_to(
        jnp.arange(half_high, dtype=jnp.int32)[None, :, None], (frames, half_high, half_wide)
    ).reshape(-1)
    query_x = jnp.broadcast_to(
        jnp.arange(half_wide, dtype=jnp.int32)[None, None, :], (frames, half_high, half_wide)
    ).reshape(-1)
    key_y = jnp.broadcast_to(
        jnp.arange(win_high, dtype=jnp.int32)[None, :, None] - span, (frames, win_high, win_wide)
    ).reshape(-1)
    key_x = jnp.broadcast_to(
        jnp.arange(win_wide, dtype=jnp.int32)[None, None, :] - span, (frames, win_high, win_wide)
    ).reshape(-1)
    band_at = jnp.array([0, 0, 1, 1], dtype=jnp.int32)
    strip_at = jnp.array([0, 1, 0, 1], dtype=jnp.int32)
    global_y = row_at * high + band_at[:, None] * half_high + key_y[None, :]
    global_x = col_at * wide + strip_at[:, None] * half_wide + key_x[None, :]
    inside = (global_y >= 0) & (global_y < grid * high) & (global_x >= 0) & (global_x < grid * wide)
    distance = jnp.maximum(
        jnp.abs(query_y[:, None] - key_y[None, :]), jnp.abs(query_x[:, None] - key_x[None, :])
    )
    near = distance[None, :, :] <= radius[:, None, None]
    allowed = near[None, :, :, :] & inside[:, None, None, :]
    scale = 1.0 / math.sqrt(head_dim)
    initial = (
        jnp.full((4, heads_here, quarter), -1e30, jnp.float32),
        jnp.zeros((4, heads_here, quarter), jnp.float32),
        jnp.zeros((4, heads_here, quarter, head_dim), jnp.float32),
    )

    def tile_move(face_key, face_value, offset):
        return passed_along((face_key, face_value), "tile", offset)

    key_all, value_all = (
        lax.all_gather(keys[0], "tm", axis=0, tiled=True),
        lax.all_gather(values[0], "tm", axis=0, tiled=True),
    )
    key_full, value_full = widen(key_all, value_all, span, tile_move, tile_move)
    stretch_ids = jnp.arange(key_full.shape[0], dtype=jnp.int32)

    def one_stretch(state, item):
        key_block, value_block, stretch_id = item
        visible = (
            lax.dynamic_slice_in_dim(
                lax.dynamic_index_in_dim(block_mask, stretch_at, 1, False), stretch_id, 1, 1
            )[:, 0]
            > 0
        )
        best, total, acc = state
        key_win = windows_of(
            key_block, half_high, half_wide, win_high, win_wide, heads_here, head_dim
        )
        value_win = windows_of(
            value_block, half_high, half_wide, win_high, win_wide, heads_here, head_dim
        )
        usable = allowed & visible[None, :, None, None]
        scores = (
            jnp.einsum("nqhd,nkhd->nhqk", queries, key_win, preferred_element_type=jnp.float32)
            * scale
        )
        masked = jnp.where(usable, scores, jnp.float32(-1e30))
        fresh = jnp.maximum(best, jnp.max(masked, axis=3))
        probs = jnp.where(usable, jnp.exp(scores - fresh[..., None]), jnp.float32(0.0))
        shrink = jnp.exp(best - fresh)
        total = total * shrink + jnp.sum(probs, axis=3)
        acc = acc * shrink[..., None] + jnp.einsum(
            "nhqk,nkhd->nhqd",
            probs.astype(jnp.bfloat16),
            value_win,
            preferred_element_type=jnp.float32,
        )
        return ((fresh, total, acc), None)

    final, unused = lax.scan(one_stretch, initial, (key_full, value_full, stretch_ids))
    best, total, acc = final
    attn = (acc / total[..., None]).astype(jnp.bfloat16)
    attn = attn.transpose(0, 2, 1, 3).reshape(
        2, 2, frames, half_high, half_wide, heads_here * head_dim
    )
    attn = attn.transpose(2, 0, 3, 1, 4, 5).reshape(tokens_here, heads_here * head_dim)
    mixed = lax.psum_scatter(
        jnp.dot(attn, out_weight, preferred_element_type=jnp.float32).astype(jnp.bfloat16),
        "head",
        scatter_dimension=0,
        tiled=True,
    )
    return mixed.reshape(1, 1, -1, out_weight.shape[1])


def tile_place():
    tile_at = lax.axis_index("tile")
    return tile_at // 2, tile_at % 2


def part_kernel(w_ref, part_ref, sem):
    tall, broad = part_ref.shape
    top = pl.multiple_of(lax.axis_index("tile") * tall, 16)
    left = pl.multiple_of(lax.axis_index("tm") * broad, 128)
    copy = pltpu.make_async_copy(w_ref.at[pl.ds(top, tall), pl.ds(left, broad)], part_ref, sem)
    copy.start()
    copy.wait()


def face_kernel(k_ref, v_ref, part_ref, row_ref, col_ref, corner_ref, tile_ref, *, geometry):
    high, wide, span, frames = geometry[:4]
    cells = high * wide
    row_at, col_at = tile_place()
    y0 = jnp.where(row_at == 0, high - span, 0)
    x0 = jnp.where(col_at == 0, wide - span, 0)

    def picker(count, cell_of):
        row = lax.broadcasted_iota(jnp.int32, (count, cells), 0)
        col = lax.broadcasted_iota(jnp.int32, (count, cells), 1)
        return (col == cell_of(row)).astype(jnp.bfloat16)

    beside = picker(high * span, lambda i: (i // span) * wide + x0 + i % span)
    across = picker(span * span, lambda i: (y0 + i // span) * wide + x0 + i % span)
    for which, ref in enumerate((k_ref, v_ref)):
        tile_ref[which] = ref[...]
        for f in range(frames):
            start = pl.multiple_of(f * cells + y0 * wide, 16)
            row_ref[which, f] = ref[pl.ds(start, span * wide)]
            whole = ref[f * cells : (f + 1) * cells]
            col_ref[which, f] = jnp.dot(
                beside, whole, preferred_element_type=jnp.float32
            ).astype(jnp.bfloat16)
            corner_ref[which, f] = jnp.dot(
                across, whole, preferred_element_type=jnp.float32
            ).astype(jnp.bfloat16)


def edge_kernel(row_ref, col_ref, corner_ref, out_ref):
    for which in range(2):
        at = 0
        for part in (row_ref, col_ref, corner_ref):
            for f in range(part.shape[1]):
                size = part.shape[2]
                out_ref[which, at : at + size] = part[which, f]
                at += size


def distances(high, wide, span, frames):
    row_at, col_at = tile_place()
    cells = high * wide
    count = frames * (cells + span * (wide + high + span))
    j = lax.broadcasted_iota(jnp.int32, (1, count), 1)
    y_off = jnp.where(row_at == 0, high, -span)
    x_off = jnp.where(col_at == 0, wide, -span)
    c = j % cells
    ky, kx = c // wide, c % wide
    base = frames * cells
    c = (j - base) % (span * wide)
    ky = jnp.where(j >= base, y_off + c // wide, ky)
    kx = jnp.where(j >= base, c % wide, kx)
    base += frames * span * wide
    c = (j - base) % (span * high)
    ky = jnp.where(j >= base, c // span, ky)
    kx = jnp.where(j >= base, x_off + c % span, kx)
    base += frames * span * high
    c = (j - base) % (span * span)
    ky = jnp.where(j >= base, y_off + c // span, ky)
    kx = jnp.where(j >= base, x_off + c % span, kx)
    i = lax.broadcasted_iota(jnp.int32, (cells, 1), 0)
    return jnp.maximum(jnp.abs(i // wide - ky), jnp.abs(i % wide - kx))


def attend(units, factor):
    scores = [
        [
            jnp.where(
                dist <= reach,
                lax.dot_general(
                    q, k, (((1,), (1,)), ((), ())), preferred_element_type=jnp.float32
                )
                * factor,
                FAR,
            )
            for k, v, dist, reach in pieces
        ]
        for q, pieces, before in units
    ]
    tops = []
    for parts, (q, pieces, before) in zip(scores, units):
        found = [jnp.max(s, axis=1, keepdims=True) for s in parts]
        if before is not None:
            found.append(before)
        tops.append(functools.reduce(jnp.maximum, found))
    probs = [
        [jnp.exp2(s - m).astype(jnp.bfloat16) for s in parts] for parts, m in zip(scores, tops)
    ]
    sums = []
    for parts, (q, pieces, before) in zip(probs, units):
        total = None
        for p, (k, v, dist, reach) in zip(parts, pieces):
            both = jnp.concatenate([v, jnp.ones_like(v)], axis=1)
            got = jnp.dot(p, both, preferred_element_type=jnp.float32)
            total = got if total is None else total + got
        sums.append(total)
    return tops, sums


def attend_tile(q_ref, tile_ref, dist_ref, reach_of, heads, state, geometry):
    high, wide, span, frames, head_dim, factor, step = geometry
    cells = high * wide
    acc_ref, sum_ref, max_ref = state
    for at, head in enumerate(heads):
        cols = slice(head * head_dim, (head + 1) * head_dim)
        outs = slice(at * head_dim, (at + 1) * head_dim)
        starts = range(0, q_ref.shape[0], step)
        units = []
        for start in starts:
            near = dist_ref[start % cells : start % cells + step, : tile_ref.shape[1]]
            piece = (tile_ref[0, :, cols], tile_ref[1, :, cols], near, reach_of(head))
            units.append((q_ref[start : start + step, cols], [piece], None))
        for start, m, got in zip(starts, *attend(units, factor)):
            rows = slice(start, start + step)
            acc_ref[rows, outs] = got[:, :head_dim]
            sum_ref[rows, outs] = got[:, head_dim:]
            max_ref[rows, outs] = jnp.broadcast_to(m, (step, head_dim))


def begin_kernel(radius_ref, mask_ref, q_ref, tile_ref, *outs, geometry, heads):
    *state, dist_ref, reach_ref = outs
    high, wide, span, frames = geometry[:4]
    dist_ref[...] = distances(high, wide, span, frames)
    stretch_at = lax.axis_index("tm")
    line = (1, reach_ref.shape[1])
    for head in range(heads):
        radius = radius_ref[head]
        seen = mask_ref[stretch_at, 0, head] > 0
        reach_ref[head : head + 1] = jnp.full(line, radius, jnp.int32)
        reach_ref[heads + head : heads + head + 1] = jnp.full(
            line, jnp.where(seen, radius, -1), jnp.int32
        )
    attend_tile(q_ref, tile_ref, dist_ref, lambda h: radius_ref[h], (0,), state, geometry)


def tile_kernel(q_ref, tile_ref, dist_ref, reach_ref, *state, geometry, heads):
    attend_tile(
        q_ref,
        tile_ref,
        dist_ref,
        lambda h: reach_ref[h : h + 1, :1],
        range(1, heads),
        state,
        geometry,
    )


def pick_state(head_state, state, head, rows, head_dim):
    refs = head_state if head == 0 else state
    at = max(head - 1, 0) * head_dim
    return [ref[rows, at : at + head_dim] for ref in refs]


def rest_kernel(
    q_ref,
    edge_ref,
    first_tile_ref,
    first_edge_ref,
    *rest,
    geometry,
    heads,
    flips,
):
    head_state, dist_ref, reach_ref, state, outs = rest[:3], rest[3], rest[4], rest[5:8], rest[8:]
    high, wide, span, frames, head_dim, factor, step = geometry
    cells = high * wide
    base = frames * cells
    head_at = lax.axis_index("head")
    stretch_at = lax.axis_index("tm")

    def run(with_first):
        for flip, out_ref in zip(flips, outs):
            start = pl.multiple_of(jnp.bitwise_xor(head_at, flip) * step, step)
            rows = pl.ds(start, step)
            near = dist_ref[pl.ds(pl.multiple_of(lax.rem(start, cells), step), step)]
            beyond = near[:, base:]
            units = []
            olds = []
            for head in range(heads):
                cols = slice(head * head_dim, (head + 1) * head_dim)
                sources = [(edge_ref, beyond, head)]
                if with_first:
                    sources.append((first_tile_ref, near[:, :base], heads + head))
                    sources.append((first_edge_ref, beyond, heads + head))
                pieces = [
                    (ref[0, :, cols], ref[1, :, cols], dist, reach_ref[row : row + 1, :1])
                    for ref, dist, row in sources
                ]
                olds.append(pick_state(head_state, state, head, rows, head_dim))
                units.append((q_ref[rows, cols], pieces, olds[-1][2][:, :1]))
            for head, (m, got) in enumerate(zip(*attend(units, factor))):
                old_acc, old_total, old_max = olds[head]
                shrink = jnp.exp2(old_max - m)
                acc = old_acc * shrink + got[:, :head_dim]
                total = old_total * shrink + got[:, head_dim:]
                cols = slice(head * head_dim, (head + 1) * head_dim)
                out_ref[:, cols] = (acc / total).astype(jnp.bfloat16)

    @pl.when(stretch_at > 0)
    def _():
        run(True)

    @pl.when(stretch_at == 0)
    def _():
        run(False)


def copy_kernel(in_ref, out_ref):
    out_ref[...] = in_ref[...]


def stack_kernel(*refs):
    *parts, out_ref = refs
    tile_at = lax.axis_index("tile")
    for flip, part in enumerate(parts):
        tall = part.shape[0]
        top = pl.multiple_of(jnp.bitwise_xor(tile_at, flip) * tall, 16)
        out_ref[pl.ds(top, tall)] = part[...]


def project_kernel(w_ref, part_ref, own_ref, got_ref, out_ref, *, flip):
    broad = part_ref.shape[1]
    half = jnp.bitwise_xor(lax.axis_index("tm"), flip)
    cols = pl.ds(pl.multiple_of(half * broad, 128), broad)
    total = jnp.dot(own_ref[...], w_ref[:, cols], preferred_element_type=jnp.float32)
    total += jnp.dot(got_ref[...], part_ref[...], preferred_element_type=jnp.float32)
    out_ref[...] = total.astype(out_ref.dtype)


def add_kernel(mine_ref, got_ref, *rest, flip):
    out_ref, sum_ref, sems = rest[-3:]
    pieces, tall, broad = sum_ref.shape
    half = jnp.bitwise_xor(lax.axis_index("tm"), flip)
    cols = pl.ds(pl.multiple_of(half * broad, 128), broad)
    copies = []
    for i in range(pieces):
        rows = slice(i * tall, (i + 1) * tall)
        sum_ref[i] = (mine_ref[rows] + got_ref[rows].astype(jnp.float32)).astype(jnp.bfloat16)
        copies.append(pltpu.make_async_copy(sum_ref.at[i], out_ref.at[rows, cols], sems.at[i]))
        copies[-1].start()
    for copy in copies:
        copy.wait()


def two_by_two(query, keys, values, out_weight, radius, block_mask):
    span = RMAX
    frames, high, wide, channels = query.shape[2:]
    heads = radius.shape[0]
    head_dim = channels // heads
    cells = high * wide
    tokens = frames * cells
    groups = lax.axis_size("head")
    tiles = lax.axis_size("tile")
    depth, width = out_weight.shape
    step = tokens // groups
    geometry = (high, wide, span, frames, head_dim, LOG2E / math.sqrt(head_dim), step)
    count = frames * (cells + span * (wide + high + span))
    smem = pl.BlockSpec(memory_space=pltpu.SMEM)
    vmem = pl.BlockSpec(memory_space=pltpu.VMEM)
    hbm = pl.BlockSpec(memory_space=pltpu.HBM)
    bf16, f32 = jnp.bfloat16, jnp.float32
    shape = jax.ShapeDtypeStruct

    def call(kernel, out_shape, specs, *args, name, scratch=(), flops=0, **keys_of):
        return pl.pallas_call(
            functools.partial(kernel, **keys_of) if keys_of else kernel,
            out_shape=out_shape,
            in_specs=specs,
            out_specs=jax.tree.map(lambda _: vmem, out_shape),
            scratch_shapes=scratch,
            cost_estimate=pl.CostEstimate(flops=flops, bytes_accessed=0, transcendentals=0),
            compiler_params=pltpu.CompilerParams(vmem_limit_bytes=VMEM_LIMIT),
            name=name,
        )(*args)

    def flipped(value, axis, flip):
        return lax.ppermute(value, axis, [(i, i ^ flip) for i in range(lax.axis_size(axis))])

    q = query.reshape(tokens, channels)
    k = keys.reshape(tokens, channels)
    v = values.reshape(tokens, channels)

    tall, broad = depth // tiles, width // 2
    part_shape = shape((tall, broad), bf16)
    part = call(
        part_kernel,
        part_shape,
        [hbm],
        pltpu.with_memory_space_constraint(out_weight, pltpu.HBM),
        name="part",
        scratch=[pltpu.SemaphoreType.DMA],
    )
    *faces, tile = call(
        face_kernel,
        [
            shape((2, frames, span * wide, channels), bf16),
            shape((2, frames, span * high, channels), bf16),
            shape((2, frames, span * span, channels), bf16),
            shape((2, tokens, channels), bf16),
        ],
        [vmem] * 3,
        k,
        v,
        part,
        name="faces",
        geometry=geometry,
    )
    faces = [flipped(face, "tile", flip) for face, flip in zip(faces, (2, 1, 3))]
    lone = flipped(part, "head", 2)
    begun = call(
        begin_kernel,
        [shape((tokens, head_dim), f32)] * 3
        + [shape((cells, count), jnp.int32), shape((2 * heads, head_dim), jnp.int32)],
        [smem] * 2 + [vmem] * 2,
        radius,
        block_mask.transpose(1, 2, 0),
        q,
        tile,
        name="begin",
        geometry=geometry,
        heads=heads,
    )
    begun, tile = lax.optimization_barrier((begun, tile))
    first_tile = lax.ppermute(tile, "tm", [(0, 1)])
    state = call(
        tile_kernel,
        [shape((tokens, channels - head_dim), f32)] * 3,
        [vmem] * 4,
        q,
        tile,
        *begun[3:],
        name="tile",
        geometry=geometry,
        heads=heads,
    )
    lone, state = lax.optimization_barrier((lone, state))
    lone = call(copy_kernel, part_shape, [vmem], lone, name="lone", flops=2 * 10**9)
    lone, state, faces = lax.optimization_barrier((lone, state, faces))
    edge = call(
        edge_kernel, shape((2, count - tokens, channels), bf16), [vmem] * 3, *faces, name="edges", flops=20 * 10**9
    )
    first_edge = lax.ppermute(edge, "tm", [(0, 1)])
    parts = [lone] + [flipped(lone, "tile", flip) for flip in range(1, tiles)]

    def rest(state, *flips, flops=0):
        return call(
            rest_kernel,
            [shape((step, channels), bf16)] * len(flips),
            [vmem] * 12,
            q,
            edge,
            first_tile,
            first_edge,
            *begun,
            *state,
            name="rest",
            geometry=geometry,
            heads=heads,
            flips=flips,
            flops=flops,
        )

    (for_side,) = rest(state, 3)
    got_side = flipped(for_side, "head", 2)
    state, for_side = lax.optimization_barrier((state, for_side))
    for_far, own_side = rest(state, 2, 1)
    parts, own_side = lax.optimization_barrier((parts, own_side))
    here = call(
        stack_kernel, shape((depth, broad), bf16), [vmem] * tiles, *parts, name="stack"
    )

    there = flipped(here, "tm", 1)

    def project(part, mine, got, kind, flip, flops=0):
        return call(
            project_kernel,
            shape((step, broad), kind),
            [vmem] * 4,
            out_weight,
            part,
            mine,
            got,
            name="project",
            flops=flops,
            flip=flip,
        )

    for_side = [project(here, own_side, got_side, bf16, 0, 20 * 10**9)]
    from_side = [flipped(for_side[0], "head", 1)]
    for_far, for_side[0] = lax.optimization_barrier((for_far, for_side[0]))
    got_far = flipped(for_far, "head", 2)
    for_side.append(project(there, own_side, got_side, bf16, 1))
    from_side.append(flipped(for_side[1], "head", 1))
    state, for_side[1] = lax.optimization_barrier((state, for_side[1]))
    (own,) = rest(state, 0, flops=20 * 10**9)
    mine = [
        project(here, own, got_far, f32, 0),
        project(there, own, got_far, f32, 1, 20 * 10**9),
    ]
    pieces = 2
    mixed = []
    for flip in range(2):
        mixed = [
            pl.pallas_call(
                functools.partial(add_kernel, flip=flip),
                out_shape=shape((step, width), bf16),
                in_specs=[vmem] * 2 + [hbm] * flip,
                out_specs=hbm,
                input_output_aliases={2: 0} if flip else {},
                scratch_shapes=[
                    pltpu.VMEM((pieces, step // pieces, broad), bf16),
                    pltpu.SemaphoreType.DMA((pieces,)),
                ],
                compiler_params=pltpu.CompilerParams(vmem_limit_bytes=VMEM_LIMIT),
                name="add",
            )(mine[flip], from_side[flip], *mixed)
        ]
    (mixed,) = mixed
    return mixed.reshape(1, 1, step, width)


def solution(mesh):
    in_specs = (
        P("tm", "tile", None, None, None, "head"),
        P("tm", "tile", None, None, None, "head"),
        P("tm", "tile", None, None, None, "head"),
        P("head", None),
        P("head"),
        P("head", None, None),
    )
    out_specs = P("tm", "tile", "head", None)
    small = dict(mesh.shape) == {"tm": 2, "tile": 4, "head": 4}
    return jax.shard_map(
        two_by_two if small else any_grid,
        mesh=mesh,
        in_specs=in_specs,
        out_specs=out_specs,
        check_vma=False,
    )
```

profile of v0, /device:TPU:0, one launch (start us, length us, event | category | flops | bytes accessed | tf_op | source)
XLA Modules:
  0.0 39.7 jit_solution(985756114749291097)
XLA Ops:
  0.0 0.0 copy-start.2
  0.0 0.0 copy-start.3
  0.0 0.0 copy-start.1
  0.0 0.0 copy-start.5
  0.0 0.0 copy-start.4
  0.0 1.0 %part.1.part_ref = bf16[96,768]{1,0:T(8,128)(2,1)S(1)} custom-call(bf16[384,1536]{1,0:T(8,128)(2,1)} %w_ref.9), custom_call_target="tpu_custom_call" | custom-call | tf_op jit(solution)/shard_map/part/pallas_call | solution.py:458
  1.0 4.1 %collective-permute-start = (bf16[96,768]{1,0:T(8,128)(2,1)S(1)}, bf16[96,768]{1,0:T(8,128)(2,1)S(1)}, u32[]{:S(2)}, u32[]{:S(2)}) collective-permute-start(bf16[96,768]{1,0:T(8,128)(2,1)S(1)} %part.1.part_ref), channel_id=1, source_target_pairs={{0,2},{1,3},{2,0},{3,1},{4,6},{5,7},{6,4},{7,5},{8,10},{9,11},{10,... | collective-permute-start | bytes 442376 | tf_op jit(solution)/shard_map/ppermute | solution.py:470
  5.2 0.0 copy-done.2
  5.2 0.0 copy-done.3
  5.2 0.4 faces.1
  5.6 1.6 %collective-permute-start.1 = (bf16[2,2,64,384]{3,2,1,0:T(8,128)(2,1)S(1)}, bf16[2,2,64,384]{3,2,1,0:T(8,128)(2,1)S(1)}, u32[]{:S(2)}, u32[]{:S(2)}) collective-permute-start(bf16[2,2,64,384]{3,2,1,0:T(8,128)(2,1)S(1)} %get-tuple-element.64), channel_id=1, source_target_pairs={{0,8},{4,12},{8,0},{12,4},{1,9},{5,13},{9,1},{13,5},{2,10},{6,14},... | collective-permute-start | bytes 589832 | tf_op jit(solution)/shard_map/ppermute | solution.py:470
  7.1 1.5 %collective-permute-start.2 = (bf16[2,2,64,384]{3,2,1,0:T(8,128)(2,1)S(1)}, bf16[2,2,64,384]{3,2,1,0:T(8,128)(2,1)S(1)}, u32[]{:S(2)}, u32[]{:S(2)}) collective-permute-start(bf16[2,2,64,384]{3,2,1,0:T(8,128)(2,1)S(1)} %get-tuple-element.65), channel_id=1, source_target_pairs={{0,4},{4,0},{8,12},{12,8},{1,5},{5,1},{9,13},{13,9},{2,6},{6,2},{1... | collective-permute-start | bytes 589832 | tf_op jit(solution)/shard_map/ppermute | solution.py:470
  8.6 0.5 %collective-permute-start.3 = (bf16[2,2,16,384]{3,2,1,0:T(8,128)(2,1)S(1)}, bf16[2,2,16,384]{3,2,1,0:T(8,128)(2,1)S(1)}, u32[]{:S(2)}, u32[]{:S(2)}) collective-permute-start(bf16[2,2,16,384]{3,2,1,0:T(8,128)(2,1)S(1)} %get-tuple-element.66), channel_id=1, source_target_pairs={{0,12},{4,8},{8,4},{12,0},{1,13},{5,9},{9,5},{13,1},{2,14},{6,10},... | collective-permute-start | bytes 147464 | tf_op jit(solution)/shard_map/ppermute | solution.py:470
  9.1 0.0 copy-done.1
  9.1 0.0 copy-done.5
  9.1 0.0 copy-done.4
  9.1 1.4 %begin.1 = (f32[512,128]{1,0:T(8,128)S(1)}, f32[512,128]{1,0:T(8,128)S(1)}, f32[512,128]{1,0:T(8,128)S(1)}, s32[256,800]{1,0:T(8,128)S(1)}, s32[6,128]{1,0:T(8,128)S(1)}) custom-call(s32[3]{0:T(128)S(1)} %copy-done.5, s32[2,2,3]{2,1,0:T(2,128)S(1)} %bitcast.12, bf16[512,384]{1,0:T(8,128)(2,1)S(1)} %bitcast.5, bf16[2,512,384]{2,1,0:T(8,128)(2,1)S(1)} %get-tuple-element.54.tile_ref), custom_call_target="tpu_custom_call" | custom-call | tf_op jit(solution)/shard_map/begin/pallas_call | solution.py:458
  10.5 1.3 %collective-permute-start.7 = (bf16[2,512,384]{2,1,0:T(8,128)(2,1)S(1)}, bf16[2,512,384]{2,1,0:T(8,128)(2,1)S(1)}, u32[]{:S(2)}, u32[]{:S(2)}) collective-permute-start(bf16[2,512,384]{2,1,0:T(8,128)(2,1)S(1)} %get-tuple-element.54.tile_ref), channel_id=1, source_target_pairs={{0,16},{1,17},{2,18},{3,19},{4,20},{5,21},{6,22},{7,23},{8,24},{9,... | collective-permute-start | bytes 2359304 | tf_op jit(solution)/shard_map/ppermute | solution.py:517
  11.9 1.1 %tile.1 = (f32[512,256]{1,0:T(8,128)S(1)}, f32[512,256]{1,0:T(8,128)S(1)}, f32[512,256]{1,0:T(8,128)S(1)}) custom-call(bf16[512,384]{1,0:T(8,128)(2,1)S(1)} %bitcast.6, bf16[2,512,384]{2,1,0:T(8,128)(2,1)S(1)} %get-tuple-element.54.tile_ref, s32[256,800]{1,0:T(8,128)S(1)} %get-tuple-element.55.dist_ref.rest_3_, s32[6,128]{1,0:T(8,128)S(1)} %get-tuple-element.56.reach_ref.rest_4_), custom_call_target="tpu_custom_call" | custom-call | tf_op jit(solution)/shard_map/tile/pallas_call | solution.py:458
  12.9 0.0 collective-permute-done.in_ref
  13.0 1.3 %collective-permute-done.3.corner_ref = bf16[2,2,16,384]{3,2,1,0:T(8,128)(2,1)S(1)} collective-permute-done((bf16[2,2,16,384]{3,2,1,0:T(8,128)(2,1)S(1)}, bf16[2,2,16,384]{3,2,1,0:T(8,128)(2,1)S(1)}, u32[]{:S(2)}, u32[]{:S(2)}) %collective-permute-start.3) | collective-permute-done | bytes 49184 | tf_op jit(solution)/shard_map/ppermute | solution.py:470
  14.2 0.0 collective-permute-done.1.row_ref
  14.2 0.0 collective-permute-done.2.col_ref
  14.3 1.3 %collective-permute-start.8 = (bf16[2,288,384]{2,1,0:T(8,128)(2,1)S(1)}, bf16[2,288,384]{2,1,0:T(8,128)(2,1)S(1)}, u32[]{:S(2)}, u32[]{:S(2)}) collective-permute-start(bf16[2,288,384]{2,1,0:T(8,128)(2,1)S(1)} %edges.1.edge_ref), channel_id=1, source_target_pairs={{0,16},{1,17},{2,18},{3,19},{4,20},{5,21},{6,22},{7,23},{8,24},{9,... | collective-permute-start | bytes 1327112 | tf_op jit(solution)/shard_map/ppermute | solution.py:535
  15.6 1.6 %collective-permute-start.4 = (bf16[96,768]{1,0:T(8,128)(2,1)S(1)}, bf16[96,768]{1,0:T(8,128)(2,1)S(1)}, u32[]{:S(2)}, u32[]{:S(2)}) collective-permute-start(bf16[96,768]{1,0:T(8,128)(2,1)S(1)} %lone.1.refs_0_), channel_id=1, source_target_pairs={{0,4},{4,0},{8,12},{12,8},{1,5},{5,1},{9,13},{13,9},{2,6},{6,2},{1... | collective-permute-start | bytes 442376 | tf_op jit(solution)/shard_map/ppermute | solution.py:470
  17.2 1.5 %collective-permute-start.5 = (bf16[96,768]{1,0:T(8,128)(2,1)S(1)}, bf16[96,768]{1,0:T(8,128)(2,1)S(1)}, u32[]{:S(2)}, u32[]{:S(2)}) collective-permute-start(bf16[96,768]{1,0:T(8,128)(2,1)S(1)} %lone.1.refs_0_), channel_id=1, source_target_pairs={{0,8},{4,12},{8,0},{12,4},{1,9},{5,13},{9,1},{13,5},{2,10},{6,14},... | collective-permute-start | bytes 442376 | tf_op jit(solution)/shard_map/ppermute | solution.py:470
  18.7 0.5 %collective-permute-start.6 = (bf16[96,768]{1,0:T(8,128)(2,1)S(1)}, bf16[96,768]{1,0:T(8,128)(2,1)S(1)}, u32[]{:S(2)}, u32[]{:S(2)}) collective-permute-start(bf16[96,768]{1,0:T(8,128)(2,1)S(1)} %lone.1.refs_0_), channel_id=1, source_target_pairs={{0,12},{4,8},{8,4},{12,0},{1,13},{5,9},{9,5},{13,1},{2,14},{6,10},... | collective-permute-start | bytes 442376 | tf_op jit(solution)/shard_map/ppermute | solution.py:470
  19.2 0.0 collective-permute-done.8.first_edge_ref
  19.2 0.0 collective-permute-done.7.first_tile_ref
  19.2 0.7 %rest.3 = bf16[128,384]{1,0:T(8,128)(2,1)S(1)} custom-call(bf16[512,384]{1,0:T(8,128)(2,1)S(1)} %bitcast.7, bf16[2,288,384]{2,1,0:T(8,128)(2,1)S(1)} %edges.1.edge_ref, bf16[2,512,384]{2,1,0:T(8,128)(2,1)S(1)} %collective-permute-done.7.first_tile_ref, bf16[2,288,384]{2,1,0:T(8,128)(2,1)S(1)} %collective-permute-done.8.first_edge_ref, ...), custom_call_target="tpu_custom_call" | custom-call | tf_op jit(solution)/shard_map/rest/pallas_call | solution.py:458
  19.8 0.4 %collective-permute-start.10 = (bf16[128,384]{1,0:T(8,128)(2,1)S(1)}, bf16[128,384]{1,0:T(8,128)(2,1)S(1)}, u32[]{:S(2)}, u32[]{:S(2)}) collective-permute-start(bf16[128,384]{1,0:T(8,128)(2,1)S(1)} %rest.3), channel_id=1, source_target_pairs={{0,2},{1,3},{2,0},{3,1},{4,6},{5,7},{6,4},{7,5},{8,10},{9,11},{10,... | collective-permute-start | bytes 294920 | tf_op jit(solution)/shard_map/ppermute | solution.py:470
  20.2 1.2 %rest.4 = (bf16[128,384]{1,0:T(8,128)(2,1)S(1)}, bf16[128,384]{1,0:T(8,128)(2,1)S(1)}) custom-call(bf16[512,384]{1,0:T(8,128)(2,1)S(1)} %bitcast.8, bf16[2,288,384]{2,1,0:T(8,128)(2,1)S(1)} %edges.1.edge_ref, bf16[2,512,384]{2,1,0:T(8,128)(2,1)S(1)} %collective-permute-done.7.first_tile_ref, bf16[2,288,384]{2,1,0:T(8,128)(2,1)S(1)} %collective-permute-done.8.first_edge_ref, ...), custom_call_target="tpu_custom_call" | custom-call | tf_op jit(solution)/shard_map/rest/pallas_call | solution.py:458
  21.4 0.0 copy-start
  21.4 0.5 %collective-permute-done.4.refs_1_ = bf16[96,768]{1,0:T(8,128)(2,1)S(1)} collective-permute-done((bf16[96,768]{1,0:T(8,128)(2,1)S(1)}, bf16[96,768]{1,0:T(8,128)(2,1)S(1)}, u32[]{:S(2)}, u32[]{:S(2)}) %collective-permute-start.4) | collective-permute-done | bytes 147488 | tf_op jit(solution)/shard_map/ppermute | solution.py:470
  21.9 1.4 %collective-permute-done.5.refs_2_ = bf16[96,768]{1,0:T(8,128)(2,1)S(1)} collective-permute-done((bf16[96,768]{1,0:T(8,128)(2,1)S(1)}, bf16[96,768]{1,0:T(8,128)(2,1)S(1)}, u32[]{:S(2)}, u32[]{:S(2)}) %collective-permute-start.5) | collective-permute-done | bytes 147488 | tf_op jit(solution)/shard_map/ppermute | solution.py:470
  23.3 1.4 %collective-permute-done.6.refs_3_ = bf16[96,768]{1,0:T(8,128)(2,1)S(1)} collective-permute-done((bf16[96,768]{1,0:T(8,128)(2,1)S(1)}, bf16[96,768]{1,0:T(8,128)(2,1)S(1)}, u32[]{:S(2)}, u32[]{:S(2)}) %collective-permute-start.6) | collective-permute-done | bytes 147488 | tf_op jit(solution)/shard_map/ppermute | solution.py:470
  24.7 0.1 stack.1.part_ref
  24.8 0.1 collective-permute-start.9
  24.9 0.5 %collective-permute-done.10.got_ref = bf16[128,384]{1,0:T(8,128)(2,1)S(1)} collective-permute-done((bf16[128,384]{1,0:T(8,128)(2,1)S(1)}, bf16[128,384]{1,0:T(8,128)(2,1)S(1)}, u32[]{:S(2)}, u32[]{:S(2)}) %collective-permute-start.10) | collective-permute-done | bytes 98336 | tf_op jit(solution)/shard_map/ppermute | solution.py:470
  25.4 0.0 copy-done
  25.4 0.4 project.5
  25.8 1.7 %collective-permute-start.13 = (bf16[128,768]{1,0:T(8,128)(2,1)S(1)}, bf16[128,768]{1,0:T(8,128)(2,1)S(1)}, u32[]{:S(2)}, u32[]{:S(2)}) collective-permute-start(bf16[128,768]{1,0:T(8,128)(2,1)S(1)} %project.5), channel_id=1, source_target_pairs={{0,1},{1,0},{2,3},{3,2},{4,5},{5,4},{6,7},{7,6},{8,9},{9,8},{10,11... | collective-permute-start | bytes 589832 | tf_op jit(solution)/shard_map/ppermute | solution.py:470
  27.5 1.4 %collective-permute-start.11 = (bf16[128,384]{1,0:T(8,128)(2,1)S(1)}, bf16[128,384]{1,0:T(8,128)(2,1)S(1)}, u32[]{:S(2)}, u32[]{:S(2)}) collective-permute-start(bf16[128,384]{1,0:T(8,128)(2,1)S(1)} %get-tuple-element.90), channel_id=1, source_target_pairs={{0,2},{1,3},{2,0},{3,1},{4,6},{5,7},{6,4},{7,5},{8,10},{9,11},{10,... | collective-permute-start | bytes 294920 | tf_op jit(solution)/shard_map/ppermute | solution.py:470
  28.9 0.0 collective-permute-done.9.part_ref
  28.9 0.4 project.4
  29.2 0.1 collective-permute-start.12
  29.4 0.7 %rest.5.own_ref = bf16[128,384]{1,0:T(8,128)(2,1)S(1)} custom-call(bf16[512,384]{1,0:T(8,128)(2,1)S(1)} %bitcast.9, bf16[2,288,384]{2,1,0:T(8,128)(2,1)S(1)} %edges.1.edge_ref, bf16[2,512,384]{2,1,0:T(8,128)(2,1)S(1)} %collective-permute-done.7.first_tile_ref, bf16[2,288,384]{2,1,0:T(8,128)(2,1)S(1)} %collective-permute-done.8.first_edge_ref, ...), custom_call_target="tpu_custom_call" | custom-call | flops 20000000000 | tf_op jit(solution)/shard_map/rest/pallas_call | solution.py:458
  30.0 4.8 %collective-permute-done.11.got_ref = bf16[128,384]{1,0:T(8,128)(2,1)S(1)} collective-permute-done((bf16[128,384]{1,0:T(8,128)(2,1)S(1)}, bf16[128,384]{1,0:T(8,128)(2,1)S(1)}, u32[]{:S(2)}, u32[]{:S(2)}) %collective-permute-start.11) | collective-permute-done | bytes 98336 | tf_op jit(solution)/shard_map/ppermute | solution.py:470
  34.9 0.4 project.6.mine_ref
  35.2 0.4 project.7.mine_ref
  35.6 0.1 collective-permute-done.13.got_ref
  35.7 0.7 %add.2.rest_0_ = bf16[128,1536]{1,0:T(8,128)(2,1)} custom-call(f32[128,768]{1,0:T(8,128)S(1)} %project.7.mine_ref, bf16[128,768]{1,0:T(8,128)(2,1)S(1)} %collective-permute-done.13.got_ref), custom_call_target="tpu_custom_call" | custom-call | tf_op jit(solution)/shard_map/add/pallas_call | solution.py:597
  36.5 2.5 %collective-permute-done.12.got_ref = bf16[128,768]{1,0:T(8,128)(2,1)S(1)} collective-permute-done((bf16[128,768]{1,0:T(8,128)(2,1)S(1)}, bf16[128,768]{1,0:T(8,128)(2,1)S(1)}, u32[]{:S(2)}, u32[]{:S(2)}) %collective-permute-start.12) | collective-permute-done | bytes 196640 | tf_op jit(solution)/shard_map/ppermute | solution.py:470
  38.9 0.7 %add.3 = bf16[128,1536]{1,0:T(8,128)(2,1)} custom-call(f32[128,768]{1,0:T(8,128)S(1)} %project.6.mine_ref, bf16[128,768]{1,0:T(8,128)(2,1)S(1)} %collective-permute-done.12.got_ref, bf16[128,1536]{1,0:T(8,128)(2,1)} %add.2.rest_0_), custom_call_target="tpu_custom_call", output_to_operand_aliasing={{}: (2, {})} | custom-call | tf_op jit(solution)/shard_map/add/pallas_call | solution.py:597
  (2 shorter events, 0.1 us)
Async XLA Ops:
  0.0 5.2 %copy-start.2 = (bf16[1,1,2,16,16,384]{5,4,3,2,1,0:T(8,128)(2,1)S(1)}, bf16[1,1,2,16,16,384]{5,4,3,2,1,0:T(8,128)(2,1)}, u32[]{:S(2)}) copy-start(bf16[1,1,2,16,16,384]{5,4,3,2,1,0:T(8,128)(2,1)} %param.7) | copy-start | bytes 1179652
  0.0 5.2 %copy-start.3 = (bf16[1,1,2,16,16,384]{5,4,3,2,1,0:T(8,128)(2,1)S(1)}, bf16[1,1,2,16,16,384]{5,4,3,2,1,0:T(8,128)(2,1)}, u32[]{:S(2)}) copy-start(bf16[1,1,2,16,16,384]{5,4,3,2,1,0:T(8,128)(2,1)} %param.8) | copy-start | bytes 1179652
  0.0 9.1 %copy-start.1 = (bf16[1,1,2,16,16,384]{5,4,3,2,1,0:T(8,128)(2,1)S(1)}, bf16[1,1,2,16,16,384]{5,4,3,2,1,0:T(8,128)(2,1)}, u32[]{:S(2)}) copy-start(bf16[1,1,2,16,16,384]{5,4,3,2,1,0:T(8,128)(2,1)} %param.6) | copy-start | bytes 1179652
  0.0 9.1 %copy-start.5 = (s32[3]{0:T(128)S(1)}, s32[3]{0:T(128)}, u32[]{:S(2)}) copy-start(s32[3]{0:T(128)} %radius_ref.1) | copy-start | bytes 40
  0.0 9.1 %copy-start.4 = (s32[3,2,2]{0,2,1:T(2,128)S(1)}, s32[3,2,2]{0,2,1:T(2,128)}, u32[]{:S(2)}) copy-start(s32[3,2,2]{0,2,1:T(2,128)} %param.11) | copy-start | bytes 148
  1.0 11.9 %collective-permute-start = (bf16[96,768]{1,0:T(8,128)(2,1)S(1)}, bf16[96,768]{1,0:T(8,128)(2,1)S(1)}, u32[]{:S(2)}, u32[]{:S(2)}) collective-permute-start(bf16[96,768]{1,0:T(8,128)(2,1)S(1)} %part.1.part_ref), channel_id=1, source_target_pairs={{0,2},{1,3},{2,0},{3,1},{4,6},{5,7},{6,4},{7,5},{8,10},{9,11},{10,... | collective-permute-start | bytes 442376 | tf_op jit(solution)/shard_map/ppermute | solution.py:470
  5.6 8.7 %collective-permute-start.1 = (bf16[2,2,64,384]{3,2,1,0:T(8,128)(2,1)S(1)}, bf16[2,2,64,384]{3,2,1,0:T(8,128)(2,1)S(1)}, u32[]{:S(2)}, u32[]{:S(2)}) collective-permute-start(bf16[2,2,64,384]{3,2,1,0:T(8,128)(2,1)S(1)} %get-tuple-element.64), channel_id=1, source_target_pairs={{0,8},{4,12},{8,0},{12,4},{1,9},{5,13},{9,1},{13,5},{2,10},{6,14},... | collective-permute-start | bytes 589832 | tf_op jit(solution)/shard_map/ppermute | solution.py:470
  7.1 7.1 %collective-permute-start.2 = (bf16[2,2,64,384]{3,2,1,0:T(8,128)(2,1)S(1)}, bf16[2,2,64,384]{3,2,1,0:T(8,128)(2,1)S(1)}, u32[]{:S(2)}, u32[]{:S(2)}) collective-permute-start(bf16[2,2,64,384]{3,2,1,0:T(8,128)(2,1)S(1)} %get-tuple-element.65), channel_id=1, source_target_pairs={{0,4},{4,0},{8,12},{12,8},{1,5},{5,1},{9,13},{13,9},{2,6},{6,2},{1... | collective-permute-start | bytes 589832 | tf_op jit(solution)/shard_map/ppermute | solution.py:470
  8.6 5.6 %collective-permute-start.3 = (bf16[2,2,16,384]{3,2,1,0:T(8,128)(2,1)S(1)}, bf16[2,2,16,384]{3,2,1,0:T(8,128)(2,1)S(1)}, u32[]{:S(2)}, u32[]{:S(2)}) collective-permute-start(bf16[2,2,16,384]{3,2,1,0:T(8,128)(2,1)S(1)} %get-tuple-element.66), channel_id=1, source_target_pairs={{0,12},{4,8},{8,4},{12,0},{1,13},{5,9},{9,5},{13,1},{2,14},{6,10},... | collective-permute-start | bytes 147464 | tf_op jit(solution)/shard_map/ppermute | solution.py:470
  10.5 8.7 %collective-permute-start.7 = (bf16[2,512,384]{2,1,0:T(8,128)(2,1)S(1)}, bf16[2,512,384]{2,1,0:T(8,128)(2,1)S(1)}, u32[]{:S(2)}, u32[]{:S(2)}) collective-permute-start(bf16[2,512,384]{2,1,0:T(8,128)(2,1)S(1)} %get-tuple-element.54.tile_ref), channel_id=1, source_target_pairs={{0,16},{1,17},{2,18},{3,19},{4,20},{5,21},{6,22},{7,23},{8,24},{9,... | collective-permute-start | bytes 2359304 | tf_op jit(solution)/shard_map/ppermute | solution.py:517
  14.3 4.9 %collective-permute-start.8 = (bf16[2,288,384]{2,1,0:T(8,128)(2,1)S(1)}, bf16[2,288,384]{2,1,0:T(8,128)(2,1)S(1)}, u32[]{:S(2)}, u32[]{:S(2)}) collective-permute-start(bf16[2,288,384]{2,1,0:T(8,128)(2,1)S(1)} %edges.1.edge_ref), channel_id=1, source_target_pairs={{0,16},{1,17},{2,18},{3,19},{4,20},{5,21},{6,22},{7,23},{8,24},{9,... | collective-permute-start | bytes 1327112 | tf_op jit(solution)/shard_map/ppermute | solution.py:535
  15.6 6.3 %collective-permute-start.4 = (bf16[96,768]{1,0:T(8,128)(2,1)S(1)}, bf16[96,768]{1,0:T(8,128)(2,1)S(1)}, u32[]{:S(2)}, u32[]{:S(2)}) collective-permute-start(bf16[96,768]{1,0:T(8,128)(2,1)S(1)} %lone.1.refs_0_), channel_id=1, source_target_pairs={{0,4},{4,0},{8,12},{12,8},{1,5},{5,1},{9,13},{13,9},{2,6},{6,2},{1... | collective-permute-start | bytes 442376 | tf_op jit(solution)/shard_map/ppermute | solution.py:470
  17.2 6.1 %collective-permute-start.5 = (bf16[96,768]{1,0:T(8,128)(2,1)S(1)}, bf16[96,768]{1,0:T(8,128)(2,1)S(1)}, u32[]{:S(2)}, u32[]{:S(2)}) collective-permute-start(bf16[96,768]{1,0:T(8,128)(2,1)S(1)} %lone.1.refs_0_), channel_id=1, source_target_pairs={{0,8},{4,12},{8,0},{12,4},{1,9},{5,13},{9,1},{13,5},{2,10},{6,14},... | collective-permute-start | bytes 442376 | tf_op jit(solution)/shard_map/ppermute | solution.py:470
  18.7 6.1 %collective-permute-start.6 = (bf16[96,768]{1,0:T(8,128)(2,1)S(1)}, bf16[96,768]{1,0:T(8,128)(2,1)S(1)}, u32[]{:S(2)}, u32[]{:S(2)}) collective-permute-start(bf16[96,768]{1,0:T(8,128)(2,1)S(1)} %lone.1.refs_0_), channel_id=1, source_target_pairs={{0,12},{4,8},{8,4},{12,0},{1,13},{5,9},{9,5},{13,1},{2,14},{6,10},... | collective-permute-start | bytes 442376 | tf_op jit(solution)/shard_map/ppermute | solution.py:470
  19.8 5.6 %collective-permute-start.10 = (bf16[128,384]{1,0:T(8,128)(2,1)S(1)}, bf16[128,384]{1,0:T(8,128)(2,1)S(1)}, u32[]{:S(2)}, u32[]{:S(2)}) collective-permute-start(bf16[128,384]{1,0:T(8,128)(2,1)S(1)} %rest.3), channel_id=1, source_target_pairs={{0,2},{1,3},{2,0},{3,1},{4,6},{5,7},{6,4},{7,5},{8,10},{9,11},{10,... | collective-permute-start | bytes 294920 | tf_op jit(solution)/shard_map/ppermute | solution.py:470
  21.4 4.0 %copy-start = (bf16[384,1536]{1,0:T(8,128)(2,1)S(1)}, bf16[384,1536]{1,0:T(8,128)(2,1)}, u32[]{:S(2)}) copy-start(bf16[384,1536]{1,0:T(8,128)(2,1)} %w_ref.9) | copy-start | bytes 3538948
  24.8 4.1 %collective-permute-start.9 = (bf16[384,768]{1,0:T(8,128)(2,1)S(1)}, bf16[384,768]{1,0:T(8,128)(2,1)S(1)}, u32[]{:S(2)}, u32[]{:S(2)}) collective-permute-start(bf16[384,768]{1,0:T(8,128)(2,1)S(1)} %stack.1.part_ref), channel_id=1, source_target_pairs={{0,16},{16,0},{1,17},{17,1},{2,18},{18,2},{3,19},{19,3},{4,20},{20... | collective-permute-start | bytes 1769480 | tf_op jit(solution)/shard_map/ppermute | solution.py:470
  25.8 9.9 %collective-permute-start.13 = (bf16[128,768]{1,0:T(8,128)(2,1)S(1)}, bf16[128,768]{1,0:T(8,128)(2,1)S(1)}, u32[]{:S(2)}, u32[]{:S(2)}) collective-permute-start(bf16[128,768]{1,0:T(8,128)(2,1)S(1)} %project.5), channel_id=1, source_target_pairs={{0,1},{1,0},{2,3},{3,2},{4,5},{5,4},{6,7},{7,6},{8,9},{9,8},{10,11... | collective-permute-start | bytes 589832 | tf_op jit(solution)/shard_map/ppermute | solution.py:470
  27.5 7.4 %collective-permute-start.11 = (bf16[128,384]{1,0:T(8,128)(2,1)S(1)}, bf16[128,384]{1,0:T(8,128)(2,1)S(1)}, u32[]{:S(2)}, u32[]{:S(2)}) collective-permute-start(bf16[128,384]{1,0:T(8,128)(2,1)S(1)} %get-tuple-element.90), channel_id=1, source_target_pairs={{0,2},{1,3},{2,0},{3,1},{4,6},{5,7},{6,4},{7,5},{8,10},{9,11},{10,... | collective-permute-start | bytes 294920 | tf_op jit(solution)/shard_map/ppermute | solution.py:470
  29.2 9.7 %collective-permute-start.12 = (bf16[128,768]{1,0:T(8,128)(2,1)S(1)}, bf16[128,768]{1,0:T(8,128)(2,1)S(1)}, u32[]{:S(2)}, u32[]{:S(2)}) collective-permute-start(bf16[128,768]{1,0:T(8,128)(2,1)S(1)} %project.4), channel_id=1, source_target_pairs={{0,1},{1,0},{2,3},{3,2},{4,5},{5,4},{6,7},{7,6},{8,9},{9,8},{10,11... | collective-permute-start | bytes 589832 | tf_op jit(solution)/shard_map/ppermute | solution.py:470
where the time goes:
time: 39.8 us; the launch traced here: 39.7 us
  starting transfers between devices  17.6 us (44%)
  waiting for transfers between devices  12.6 us (32%)
  Pallas kernels  9.3 us (23%)
    ppermute x12, starting transfers between devices, flipped(): lax.ppermute(value, axis, [(i, i ^ flip) for i in range(lax.axis_size(axi...  14.9 us
    ppermute x12, waiting for transfers between devices, flipped(): lax.ppermute(value, axis, [(i, i ^ flip) for i in range(lax.axis_size(axi...  12.6 us
    pallas_call x14, Pallas kernels, call(): pl.pallas_call(functools.partial(kernel, **keys_of) if keys_of else kerne...  7.87 us
    pallas_call x2, Pallas kernels, two_by_two(): pl.pallas_call(functools.partial(add_kernel, flip=flip), out_shape=shape(...  1.42 us
    ppermute x1, starting transfers between devices, two_by_two(): first_tile = lax.ppermute(tile, 'tm', [(0, 1)])  1.34 us
    ppermute x1, starting transfers between devices, two_by_two(): first_edge = lax.ppermute(edge, 'tm', [(0, 1)])  1.32 us
  transfers between devices with their start and end apart: 14, of which 8 were waited for; matrix products, arithmetic and copies ran while one was open for 0% of the time, Pallas kernels for 19%

commit v1 on v0

--- a/solution.py
+++ b/solution.py
@@ -556,7 +556,10 @@
     (for_side,) = rest(state, 3)
     got_side = flipped(for_side, "head", 2)
     state, for_side = lax.optimization_barrier((state, for_side))
-    for_far, own_side = rest(state, 2, 1)
+    (for_far,) = rest(state, 2)
+    got_far = flipped(for_far, "head", 2)
+    state, for_far = lax.optimization_barrier((state, for_far))
+    (own_side,) = rest(state, 1)
     parts, own_side = lax.optimization_barrier((parts, own_side))
     here = call(
         stack_kernel, shape((depth, broad), bf16), [vmem] * tiles, *parts, name="stack"
@@ -580,8 +583,6 @@
 
     for_side = [project(here, own_side, got_side, bf16, 0, 20 * 10**9)]
     from_side = [flipped(for_side[0], "head", 1)]
-    for_far, for_side[0] = lax.optimization_barrier((for_far, for_side[0]))
-    got_far = flipped(for_far, "head", 2)
     for_side.append(project(there, own_side, got_side, bf16, 1))
     from_side.append(flipped(for_side[1], "head", 1))
     state, for_side[1] = lax.optimization_barrier((state, for_side[1]))

time: 39.8 us -> 39.7 us (level)
  waiting for transfers between devices: 12.6 us -> 10.7 us
  starting transfers between devices: 17.6 us -> 19.1 us
    ppermute x12, waiting for transfers between devices: 12.6 us -> 10.7 us  [flipped(): lax.ppermute(value, axis, [(i, i ^ flip) for i in range(lax.axis_size(axi...]
    ppermute x12, starting transfers between devices: 14.9 us -> 16.5 us  [flipped(): lax.ppermute(value, axis, [(i, i ^ flip) for i in range(lax.axis_size(axi...]
    pallas_call x14 -> x15, Pallas kernels: 7.87 us -> 8.04 us  [call(): pl.pallas_call(functools.partial(kernel, **keys_of) if keys_of else kerne...]
  transfers between devices with their start and end apart: 14 -> 14, of which waited for: 8 -> 5; matrix products, arithmetic and copies ran while one was open for 0% -> 0% of each run, Pallas kernels for 19% -> 20%
where the time goes in v1:
time: 39.7 us; the launch traced here: 39.6 us
  starting transfers between devices  19.1 us (48%)
  waiting for transfers between devices  10.7 us (27%)
  Pallas kernels  9.47 us (24%)
    ppermute x12, starting transfers between devices, flipped(): lax.ppermute(value, axis, [(i, i ^ flip) for i in range(lax.axis_size(axi...  16.5 us
    ppermute x12, waiting for transfers between devices, flipped(): lax.ppermute(value, axis, [(i, i ^ flip) for i in range(lax.axis_size(axi...  10.7 us
    pallas_call x15, Pallas kernels, call(): pl.pallas_call(functools.partial(kernel, **keys_of) if keys_of else kerne...  8.04 us
    pallas_call x2, Pallas kernels, two_by_two(): pl.pallas_call(functools.partial(add_kernel, flip=flip), out_shape=shape(...  1.43 us
    ppermute x1, starting transfers between devices, two_by_two(): first_tile = lax.ppermute(tile, 'tm', [(0, 1)])  1.34 us
    ppermute x1, starting transfers between devices, two_by_two(): first_edge = lax.ppermute(edge, 'tm', [(0, 1)])  1.32 us
  transfers between devices with their start and end apart: 14, of which 5 were waited for; matrix products, arithmetic and copies ran while one was open for 0% of the time, Pallas kernels for 20%

profile of v1, /device:TPU:0, one launch (start us, length us, event | category | flops | bytes accessed | tf_op | source)
XLA Modules:
  0.0 39.6 jit_solution(1247652643863385109)
XLA Ops:
  0.0 0.0 copy-start.2
  0.0 0.0 copy-start.3
  0.0 0.0 copy-start.1
  0.0 0.0 copy-start.5
  0.0 0.0 copy-start.4
  0.0 1.0 %part.1.part_ref = bf16[96,768]{1,0:T(8,128)(2,1)S(1)} custom-call(bf16[384,1536]{1,0:T(8,128)(2,1)} %w_ref.9), custom_call_target="tpu_custom_call" | custom-call | tf_op jit(solution)/shard_map/part/pallas_call | solution.py:458
  1.0 4.1 %collective-permute-start = (bf16[96,768]{1,0:T(8,128)(2,1)S(1)}, bf16[96,768]{1,0:T(8,128)(2,1)S(1)}, u32[]{:S(2)}, u32[]{:S(2)}) collective-permute-start(bf16[96,768]{1,0:T(8,128)(2,1)S(1)} %part.1.part_ref), channel_id=1, source_target_pairs={{0,2},{1,3},{2,0},{3,1},{4,6},{5,7},{6,4},{7,5},{8,10},{9,11},{10,... | collective-permute-start | bytes 442376 | tf_op jit(solution)/shard_map/ppermute | solution.py:470
  5.2 0.0 copy-done.2
  5.2 0.0 copy-done.3
  5.2 0.4 faces.1
  5.6 1.6 %collective-permute-start.1 = (bf16[2,2,64,384]{3,2,1,0:T(8,128)(2,1)S(1)}, bf16[2,2,64,384]{3,2,1,0:T(8,128)(2,1)S(1)}, u32[]{:S(2)}, u32[]{:S(2)}) collective-permute-start(bf16[2,2,64,384]{3,2,1,0:T(8,128)(2,1)S(1)} %get-tuple-element.64), channel_id=1, source_target_pairs={{0,8},{4,12},{8,0},{12,4},{1,9},{5,13},{9,1},{13,5},{2,10},{6,14},... | collective-permute-start | bytes 589832 | tf_op jit(solution)/shard_map/ppermute | solution.py:470
  7.1 1.5 %collective-permute-start.2 = (bf16[2,2,64,384]{3,2,1,0:T(8,128)(2,1)S(1)}, bf16[2,2,64,384]{3,2,1,0:T(8,128)(2,1)S(1)}, u32[]{:S(2)}, u32[]{:S(2)}) collective-permute-start(bf16[2,2,64,384]{3,2,1,0:T(8,128)(2,1)S(1)} %get-tuple-element.65), channel_id=1, source_target_pairs={{0,4},{4,0},{8,12},{12,8},{1,5},{5,1},{9,13},{13,9},{2,6},{6,2},{1... | collective-permute-start | bytes 589832 | tf_op jit(solution)/shard_map/ppermute | solution.py:470
  8.6 0.5 %collective-permute-start.3 = (bf16[2,2,16,384]{3,2,1,0:T(8,128)(2,1)S(1)}, bf16[2,2,16,384]{3,2,1,0:T(8,128)(2,1)S(1)}, u32[]{:S(2)}, u32[]{:S(2)}) collective-permute-start(bf16[2,2,16,384]{3,2,1,0:T(8,128)(2,1)S(1)} %get-tuple-element.66), channel_id=1, source_target_pairs={{0,12},{4,8},{8,4},{12,0},{1,13},{5,9},{9,5},{13,1},{2,14},{6,10},... | collective-permute-start | bytes 147464 | tf_op jit(solution)/shard_map/ppermute | solution.py:470
  9.1 0.0 copy-done.1
  9.1 0.0 copy-done.5
  9.1 0.0 copy-done.4
  9.1 1.4 %begin.1 = (f32[512,128]{1,0:T(8,128)S(1)}, f32[512,128]{1,0:T(8,128)S(1)}, f32[512,128]{1,0:T(8,128)S(1)}, s32[256,800]{1,0:T(8,128)S(1)}, s32[6,128]{1,0:T(8,128)S(1)}) custom-call(s32[3]{0:T(128)S(1)} %copy-done.5, s32[2,2,3]{2,1,0:T(2,128)S(1)} %bitcast.13, bf16[512,384]{1,0:T(8,128)(2,1)S(1)} %bitcast.5, bf16[2,512,384]{2,1,0:T(8,128)(2,1)S(1)} %get-tuple-element.54.tile_ref), custom_call_target="tpu_custom_call" | custom-call | tf_op jit(solution)/shard_map/begin/pallas_call | solution.py:458
  10.5 1.3 %collective-permute-start.7 = (bf16[2,512,384]{2,1,0:T(8,128)(2,1)S(1)}, bf16[2,512,384]{2,1,0:T(8,128)(2,1)S(1)}, u32[]{:S(2)}, u32[]{:S(2)}) collective-permute-start(bf16[2,512,384]{2,1,0:T(8,128)(2,1)S(1)} %get-tuple-element.54.tile_ref), channel_id=1, source_target_pairs={{0,16},{1,17},{2,18},{3,19},{4,20},{5,21},{6,22},{7,23},{8,24},{9,... | collective-permute-start | bytes 2359304 | tf_op jit(solution)/shard_map/ppermute | solution.py:517
  11.9 1.1 %tile.1 = (f32[512,256]{1,0:T(8,128)S(1)}, f32[512,256]{1,0:T(8,128)S(1)}, f32[512,256]{1,0:T(8,128)S(1)}) custom-call(bf16[512,384]{1,0:T(8,128)(2,1)S(1)} %bitcast.6, bf16[2,512,384]{2,1,0:T(8,128)(2,1)S(1)} %get-tuple-element.54.tile_ref, s32[256,800]{1,0:T(8,128)S(1)} %get-tuple-element.55.dist_ref.rest_3_, s32[6,128]{1,0:T(8,128)S(1)} %get-tuple-element.56.reach_ref.rest_4_), custom_call_target="tpu_custom_call" | custom-call | tf_op jit(solution)/shard_map/tile/pallas_call | solution.py:458
  12.9 0.0 collective-permute-done.in_ref
  13.0 1.3 %collective-permute-done.3.corner_ref = bf16[2,2,16,384]{3,2,1,0:T(8,128)(2,1)S(1)} collective-permute-done((bf16[2,2,16,384]{3,2,1,0:T(8,128)(2,1)S(1)}, bf16[2,2,16,384]{3,2,1,0:T(8,128)(2,1)S(1)}, u32[]{:S(2)}, u32[]{:S(2)}) %collective-permute-start.3) | collective-permute-done | bytes 49184 | tf_op jit(solution)/shard_map/ppermute | solution.py:470
  14.2 0.0 collective-permute-done.1.row_ref
  14.2 0.0 collective-permute-done.2.col_ref
  14.3 1.3 %collective-permute-start.8 = (bf16[2,288,384]{2,1,0:T(8,128)(2,1)S(1)}, bf16[2,288,384]{2,1,0:T(8,128)(2,1)S(1)}, u32[]{:S(2)}, u32[]{:S(2)}) collective-permute-start(bf16[2,288,384]{2,1,0:T(8,128)(2,1)S(1)} %edges.1.edge_ref), channel_id=1, source_target_pairs={{0,16},{1,17},{2,18},{3,19},{4,20},{5,21},{6,22},{7,23},{8,24},{9,... | collective-permute-start | bytes 1327112 | tf_op jit(solution)/shard_map/ppermute | solution.py:535
  15.6 1.6 %collective-permute-start.4 = (bf16[96,768]{1,0:T(8,128)(2,1)S(1)}, bf16[96,768]{1,0:T(8,128)(2,1)S(1)}, u32[]{:S(2)}, u32[]{:S(2)}) collective-permute-start(bf16[96,768]{1,0:T(8,128)(2,1)S(1)} %lone.1.refs_0_), channel_id=1, source_target_pairs={{0,4},{4,0},{8,12},{12,8},{1,5},{5,1},{9,13},{13,9},{2,6},{6,2},{1... | collective-permute-start | bytes 442376 | tf_op jit(solution)/shard_map/ppermute | solution.py:470
  17.2 1.5 %collective-permute-start.5 = (bf16[96,768]{1,0:T(8,128)(2,1)S(1)}, bf16[96,768]{1,0:T(8,128)(2,1)S(1)}, u32[]{:S(2)}, u32[]{:S(2)}) collective-permute-start(bf16[96,768]{1,0:T(8,128)(2,1)S(1)} %lone.1.refs_0_), channel_id=1, source_target_pairs={{0,8},{4,12},{8,0},{12,4},{1,9},{5,13},{9,1},{13,5},{2,10},{6,14},... | collective-permute-start | bytes 442376 | tf_op jit(solution)/shard_map/ppermute | solution.py:470
  18.7 0.5 %collective-permute-start.6 = (bf16[96,768]{1,0:T(8,128)(2,1)S(1)}, bf16[96,768]{1,0:T(8,128)(2,1)S(1)}, u32[]{:S(2)}, u32[]{:S(2)}) collective-permute-start(bf16[96,768]{1,0:T(8,128)(2,1)S(1)} %lone.1.refs_0_), channel_id=1, source_target_pairs={{0,12},{4,8},{8,4},{12,0},{1,13},{5,9},{9,5},{13,1},{2,14},{6,10},... | collective-permute-start | bytes 442376 | tf_op jit(solution)/shard_map/ppermute | solution.py:470
  19.2 0.0 collective-permute-done.8.first_edge_ref
  19.2 0.0 collective-permute-done.7.first_tile_ref
  19.2 0.7 %rest.4 = bf16[128,384]{1,0:T(8,128)(2,1)S(1)} custom-call(bf16[512,384]{1,0:T(8,128)(2,1)S(1)} %bitcast.7, bf16[2,288,384]{2,1,0:T(8,128)(2,1)S(1)} %edges.1.edge_ref, bf16[2,512,384]{2,1,0:T(8,128)(2,1)S(1)} %collective-permute-done.7.first_tile_ref, bf16[2,288,384]{2,1,0:T(8,128)(2,1)S(1)} %collective-permute-done.8.first_edge_ref, ...), custom_call_target="tpu_custom_call" | custom-call | tf_op jit(solution)/shard_map/rest/pallas_call | solution.py:458
  19.8 0.4 %collective-permute-start.10 = (bf16[128,384]{1,0:T(8,128)(2,1)S(1)}, bf16[128,384]{1,0:T(8,128)(2,1)S(1)}, u32[]{:S(2)}, u32[]{:S(2)}) collective-permute-start(bf16[128,384]{1,0:T(8,128)(2,1)S(1)} %rest.4), channel_id=1, source_target_pairs={{0,2},{1,3},{2,0},{3,1},{4,6},{5,7},{6,4},{7,5},{8,10},{9,11},{10,... | collective-permute-start | bytes 294920 | tf_op jit(solution)/shard_map/ppermute | solution.py:470
  20.2 0.7 %rest.5 = bf16[128,384]{1,0:T(8,128)(2,1)S(1)} custom-call(bf16[512,384]{1,0:T(8,128)(2,1)S(1)} %bitcast.8, bf16[2,288,384]{2,1,0:T(8,128)(2,1)S(1)} %edges.1.edge_ref, bf16[2,512,384]{2,1,0:T(8,128)(2,1)S(1)} %collective-permute-done.7.first_tile_ref, bf16[2,288,384]{2,1,0:T(8,128)(2,1)S(1)} %collective-permute-done.8.first_edge_ref, ...), custom_call_target="tpu_custom_call" | custom-call | tf_op jit(solution)/shard_map/rest/pallas_call | solution.py:458
  20.9 2.7 %collective-permute-start.11 = (bf16[128,384]{1,0:T(8,128)(2,1)S(1)}, bf16[128,384]{1,0:T(8,128)(2,1)S(1)}, u32[]{:S(2)}, u32[]{:S(2)}) collective-permute-start(bf16[128,384]{1,0:T(8,128)(2,1)S(1)} %rest.5), channel_id=1, source_target_pairs={{0,2},{1,3},{2,0},{3,1},{4,6},{5,7},{6,4},{7,5},{8,10},{9,11},{10,... | collective-permute-start | bytes 294920 | tf_op jit(solution)/shard_map/ppermute | solution.py:470
  23.5 0.7 %rest.6.own_ref = bf16[128,384]{1,0:T(8,128)(2,1)S(1)} custom-call(bf16[512,384]{1,0:T(8,128)(2,1)S(1)} %bitcast.9, bf16[2,288,384]{2,1,0:T(8,128)(2,1)S(1)} %edges.1.edge_ref, bf16[2,512,384]{2,1,0:T(8,128)(2,1)S(1)} %collective-permute-done.7.first_tile_ref, bf16[2,288,384]{2,1,0:T(8,128)(2,1)S(1)} %collective-permute-done.8.first_edge_ref, ...), custom_call_target="tpu_custom_call" | custom-call | tf_op jit(solution)/shard_map/rest/pallas_call | solution.py:458
  24.2 0.0 copy-start
  24.2 0.0 collective-permute-done.4.refs_1_
  24.2 0.0 collective-permute-done.5.refs_2_
  24.2 0.5 %collective-permute-done.6.refs_3_ = bf16[96,768]{1,0:T(8,128)(2,1)S(1)} collective-permute-done((bf16[96,768]{1,0:T(8,128)(2,1)S(1)}, bf16[96,768]{1,0:T(8,128)(2,1)S(1)}, u32[]{:S(2)}, u32[]{:S(2)}) %collective-permute-start.6) | collective-permute-done | bytes 147488 | tf_op jit(solution)/shard_map/ppermute | solution.py:470
  24.7 0.1 stack.1.part_ref
  24.8 0.1 collective-permute-start.9
  24.9 4.8 %collective-permute-done.10.got_ref = bf16[128,384]{1,0:T(8,128)(2,1)S(1)} collective-permute-done((bf16[128,384]{1,0:T(8,128)(2,1)S(1)}, bf16[128,384]{1,0:T(8,128)(2,1)S(1)}, u32[]{:S(2)}, u32[]{:S(2)}) %collective-permute-start.10) | collective-permute-done | bytes 98336 | tf_op jit(solution)/shard_map/ppermute | solution.py:470
  29.7 0.0 copy-done
  29.7 0.4 project.7
  30.1 0.1 collective-permute-start.13
  30.1 0.0 collective-permute-done.9.part_ref
  30.1 0.4 project.4
  30.5 2.1 %collective-permute-start.12 = (bf16[128,768]{1,0:T(8,128)(2,1)S(1)}, bf16[128,768]{1,0:T(8,128)(2,1)S(1)}, u32[]{:S(2)}, u32[]{:S(2)}) collective-permute-start(bf16[128,768]{1,0:T(8,128)(2,1)S(1)} %project.4), channel_id=1, source_target_pairs={{0,1},{1,0},{2,3},{3,2},{4,5},{5,4},{6,7},{7,6},{8,9},{9,8},{10,11... | collective-permute-start | bytes 589832 | tf_op jit(solution)/shard_map/ppermute | solution.py:470
  32.6 0.7 %rest.7.own_ref = bf16[128,384]{1,0:T(8,128)(2,1)S(1)} custom-call(bf16[512,384]{1,0:T(8,128)(2,1)S(1)} %bitcast.10, bf16[2,288,384]{2,1,0:T(8,128)(2,1)S(1)} %edges.1.edge_ref, bf16[2,512,384]{2,1,0:T(8,128)(2,1)S(1)} %collective-permute-done.7.first_tile_ref, bf16[2,288,384]{2,1,0:T(8,128)(2,1)S(1)} %collective-permute-done.8.first_edge_ref, ...), custom_call_target="tpu_custom_call" | custom-call | flops 20000000000 | tf_op jit(solution)/shard_map/rest/pallas_call | solution.py:458
  33.2 0.0 collective-permute-done.11.got_ref
  33.2 0.4 project.5.mine_ref
  33.6 0.4 project.6.mine_ref
  34.0 2.8 %collective-permute-done.13.got_ref = bf16[128,768]{1,0:T(8,128)(2,1)S(1)} collective-permute-done((bf16[128,768]{1,0:T(8,128)(2,1)S(1)}, bf16[128,768]{1,0:T(8,128)(2,1)S(1)}, u32[]{:S(2)}, u32[]{:S(2)}) %collective-permute-start.13) | collective-permute-done | bytes 196640 | tf_op jit(solution)/shard_map/ppermute | solution.py:470
  36.7 0.7 %add.2.rest_0_ = bf16[128,1536]{1,0:T(8,128)(2,1)} custom-call(f32[128,768]{1,0:T(8,128)S(1)} %project.6.mine_ref, bf16[128,768]{1,0:T(8,128)(2,1)S(1)} %collective-permute-done.13.got_ref), custom_call_target="tpu_custom_call" | custom-call | tf_op jit(solution)/shard_map/add/pallas_call | solution.py:598
  37.5 1.4 %collective-permute-done.12.got_ref = bf16[128,768]{1,0:T(8,128)(2,1)S(1)} collective-permute-done((bf16[128,768]{1,0:T(8,128)(2,1)S(1)}, bf16[128,768]{1,0:T(8,128)(2,1)S(1)}, u32[]{:S(2)}, u32[]{:S(2)}) %collective-permute-start.12) | collective-permute-done | bytes 196640 | tf_op jit(solution)/shard_map/ppermute | solution.py:470
  38.8 0.7 %add.3 = bf16[128,1536]{1,0:T(8,128)(2,1)} custom-call(f32[128,768]{1,0:T(8,128)S(1)} %project.5.mine_ref, bf16[128,768]{1,0:T(8,128)(2,1)S(1)} %collective-permute-done.12.got_ref, bf16[128,1536]{1,0:T(8,128)(2,1)} %add.2.rest_0_), custom_call_target="tpu_custom_call", output_to_operand_aliasing={{}: (2, {})} | custom-call | tf_op jit(solution)/shard_map/add/pallas_call | solution.py:598
  (2 shorter events, 0.1 us)
Async XLA Ops:
  0.0 5.2 %copy-start.2 = (bf16[1,1,2,16,16,384]{5,4,3,2,1,0:T(8,128)(2,1)S(1)}, bf16[1,1,2,16,16,384]{5,4,3,2,1,0:T(8,128)(2,1)}, u32[]{:S(2)}) copy-start(bf16[1,1,2,16,16,384]{5,4,3,2,1,0:T(8,128)(2,1)} %param.7) | copy-start | bytes 1179652
  0.0 5.2 %copy-start.3 = (bf16[1,1,2,16,16,384]{5,4,3,2,1,0:T(8,128)(2,1)S(1)}, bf16[1,1,2,16,16,384]{5,4,3,2,1,0:T(8,128)(2,1)}, u32[]{:S(2)}) copy-start(bf16[1,1,2,16,16,384]{5,4,3,2,1,0:T(8,128)(2,1)} %param.8) | copy-start | bytes 1179652
  0.0 9.1 %copy-start.1 = (bf16[1,1,2,16,16,384]{5,4,3,2,1,0:T(8,128)(2,1)S(1)}, bf16[1,1,2,16,16,384]{5,4,3,2,1,0:T(8,128)(2,1)}, u32[]{:S(2)}) copy-start(bf16[1,1,2,16,16,384]{5,4,3,2,1,0:T(8,128)(2,1)} %param.6) | copy-start | bytes 1179652
  0.0 9.1 %copy-start.5 = (s32[3]{0:T(128)S(1)}, s32[3]{0:T(128)}, u32[]{:S(2)}) copy-start(s32[3]{0:T(128)} %radius_ref.1) | copy-start | bytes 40
  0.0 9.1 %copy-start.4 = (s32[3,2,2]{0,2,1:T(2,128)S(1)}, s32[3,2,2]{0,2,1:T(2,128)}, u32[]{:S(2)}) copy-start(s32[3,2,2]{0,2,1:T(2,128)} %param.11) | copy-start | bytes 148
  1.0 11.9 %collective-permute-start = (bf16[96,768]{1,0:T(8,128)(2,1)S(1)}, bf16[96,768]{1,0:T(8,128)(2,1)S(1)}, u32[]{:S(2)}, u32[]{:S(2)}) collective-permute-start(bf16[96,768]{1,0:T(8,128)(2,1)S(1)} %part.1.part_ref), channel_id=1, source_target_pairs={{0,2},{1,3},{2,0},{3,1},{4,6},{5,7},{6,4},{7,5},{8,10},{9,11},{10,... | collective-permute-start | bytes 442376 | tf_op jit(solution)/shard_map/ppermute | solution.py:470
  5.6 8.7 %collective-permute-start.1 = (bf16[2,2,64,384]{3,2,1,0:T(8,128)(2,1)S(1)}, bf16[2,2,64,384]{3,2,1,0:T(8,128)(2,1)S(1)}, u32[]{:S(2)}, u32[]{:S(2)}) collective-permute-start(bf16[2,2,64,384]{3,2,1,0:T(8,128)(2,1)S(1)} %get-tuple-element.64), channel_id=1, source_target_pairs={{0,8},{4,12},{8,0},{12,4},{1,9},{5,13},{9,1},{13,5},{2,10},{6,14},... | collective-permute-start | bytes 589832 | tf_op jit(solution)/shard_map/ppermute | solution.py:470
  7.1 7.1 %collective-permute-start.2 = (bf16[2,2,64,384]{3,2,1,0:T(8,128)(2,1)S(1)}, bf16[2,2,64,384]{3,2,1,0:T(8,128)(2,1)S(1)}, u32[]{:S(2)}, u32[]{:S(2)}) collective-permute-start(bf16[2,2,64,384]{3,2,1,0:T(8,128)(2,1)S(1)} %get-tuple-element.65), channel_id=1, source_target_pairs={{0,4},{4,0},{8,12},{12,8},{1,5},{5,1},{9,13},{13,9},{2,6},{6,2},{1... | collective-permute-start | bytes 589832 | tf_op jit(solution)/shard_map/ppermute | solution.py:470
  8.6 5.6 %collective-permute-start.3 = (bf16[2,2,16,384]{3,2,1,0:T(8,128)(2,1)S(1)}, bf16[2,2,16,384]{3,2,1,0:T(8,128)(2,1)S(1)}, u32[]{:S(2)}, u32[]{:S(2)}) collective-permute-start(bf16[2,2,16,384]{3,2,1,0:T(8,128)(2,1)S(1)} %get-tuple-element.66), channel_id=1, source_target_pairs={{0,12},{4,8},{8,4},{12,0},{1,13},{5,9},{9,5},{13,1},{2,14},{6,10},... | collective-permute-start | bytes 147464 | tf_op jit(solution)/shard_map/ppermute | solution.py:470
  10.5 8.7 %collective-permute-start.7 = (bf16[2,512,384]{2,1,0:T(8,128)(2,1)S(1)}, bf16[2,512,384]{2,1,0:T(8,128)(2,1)S(1)}, u32[]{:S(2)}, u32[]{:S(2)}) collective-permute-start(bf16[2,512,384]{2,1,0:T(8,128)(2,1)S(1)} %get-tuple-element.54.tile_ref), channel_id=1, source_target_pairs={{0,16},{1,17},{2,18},{3,19},{4,20},{5,21},{6,22},{7,23},{8,24},{9,... | collective-permute-start | bytes 2359304 | tf_op jit(solution)/shard_map/ppermute | solution.py:517
  14.3 4.9 %collective-permute-start.8 = (bf16[2,288,384]{2,1,0:T(8,128)(2,1)S(1)}, bf16[2,288,384]{2,1,0:T(8,128)(2,1)S(1)}, u32[]{:S(2)}, u32[]{:S(2)}) collective-permute-start(bf16[2,288,384]{2,1,0:T(8,128)(2,1)S(1)} %edges.1.edge_ref), channel_id=1, source_target_pairs={{0,16},{1,17},{2,18},{3,19},{4,20},{5,21},{6,22},{7,23},{8,24},{9,... | collective-permute-start | bytes 1327112 | tf_op jit(solution)/shard_map/ppermute | solution.py:535
  15.6 8.6 %collective-permute-start.4 = (bf16[96,768]{1,0:T(8,128)(2,1)S(1)}, bf16[96,768]{1,0:T(8,128)(2,1)S(1)}, u32[]{:S(2)}, u32[]{:S(2)}) collective-permute-start(bf16[96,768]{1,0:T(8,128)(2,1)S(1)} %lone.1.refs_0_), channel_id=1, source_target_pairs={{0,4},{4,0},{8,12},{12,8},{1,5},{5,1},{9,13},{13,9},{2,6},{6,2},{1... | collective-permute-start | bytes 442376 | tf_op jit(solution)/shard_map/ppermute | solution.py:470
  17.2 7.1 %collective-permute-start.5 = (bf16[96,768]{1,0:T(8,128)(2,1)S(1)}, bf16[96,768]{1,0:T(8,128)(2,1)S(1)}, u32[]{:S(2)}, u32[]{:S(2)}) collective-permute-start(bf16[96,768]{1,0:T(8,128)(2,1)S(1)} %lone.1.refs_0_), channel_id=1, source_target_pairs={{0,8},{4,12},{8,0},{12,4},{1,9},{5,13},{9,1},{13,5},{2,10},{6,14},... | collective-permute-start | bytes 442376 | tf_op jit(solution)/shard_map/ppermute | solution.py:470
  18.7 6.1 %collective-permute-start.6 = (bf16[96,768]{1,0:T(8,128)(2,1)S(1)}, bf16[96,768]{1,0:T(8,128)(2,1)S(1)}, u32[]{:S(2)}, u32[]{:S(2)}) collective-permute-start(bf16[96,768]{1,0:T(8,128)(2,1)S(1)} %lone.1.refs_0_), channel_id=1, source_target_pairs={{0,12},{4,8},{8,4},{12,0},{1,13},{5,9},{9,5},{13,1},{2,14},{6,10},... | collective-permute-start | bytes 442376 | tf_op jit(solution)/shard_map/ppermute | solution.py:470
  19.8 9.9 %collective-permute-start.10 = (bf16[128,384]{1,0:T(8,128)(2,1)S(1)}, bf16[128,384]{1,0:T(8,128)(2,1)S(1)}, u32[]{:S(2)}, u32[]{:S(2)}) collective-permute-start(bf16[128,384]{1,0:T(8,128)(2,1)S(1)} %rest.4), channel_id=1, source_target_pairs={{0,2},{1,3},{2,0},{3,1},{4,6},{5,7},{6,4},{7,5},{8,10},{9,11},{10,... | collective-permute-start | bytes 294920 | tf_op jit(solution)/shard_map/ppermute | solution.py:470
  20.9 12.3 %collective-permute-start.11 = (bf16[128,384]{1,0:T(8,128)(2,1)S(1)}, bf16[128,384]{1,0:T(8,128)(2,1)S(1)}, u32[]{:S(2)}, u32[]{:S(2)}) collective-permute-start(bf16[128,384]{1,0:T(8,128)(2,1)S(1)} %rest.5), channel_id=1, source_target_pairs={{0,2},{1,3},{2,0},{3,1},{4,6},{5,7},{6,4},{7,5},{8,10},{9,11},{10,... | collective-permute-start | bytes 294920 | tf_op jit(solution)/shard_map/ppermute | solution.py:470
  24.2 5.5 %copy-start = (bf16[384,1536]{1,0:T(8,128)(2,1)S(1)}, bf16[384,1536]{1,0:T(8,128)(2,1)}, u32[]{:S(2)}) copy-start(bf16[384,1536]{1,0:T(8,128)(2,1)} %w_ref.9) | copy-start | bytes 3538948
  24.8 5.3 %collective-permute-start.9 = (bf16[384,768]{1,0:T(8,128)(2,1)S(1)}, bf16[384,768]{1,0:T(8,128)(2,1)S(1)}, u32[]{:S(2)}, u32[]{:S(2)}) collective-permute-start(bf16[384,768]{1,0:T(8,128)(2,1)S(1)} %stack.1.part_ref), channel_id=1, source_target_pairs={{0,16},{16,0},{1,17},{17,1},{2,18},{18,2},{3,19},{19,3},{4,20},{20... | collective-permute-start | bytes 1769480 | tf_op jit(solution)/shard_map/ppermute | solution.py:470
  30.1 6.7 %collective-permute-start.13 = (bf16[128,768]{1,0:T(8,128)(2,1)S(1)}, bf16[128,768]{1,0:T(8,128)(2,1)S(1)}, u32[]{:S(2)}, u32[]{:S(2)}) collective-permute-start(bf16[128,768]{1,0:T(8,128)(2,1)S(1)} %project.7), channel_id=1, source_target_pairs={{0,1},{1,0},{2,3},{3,2},{4,5},{5,4},{6,7},{7,6},{8,9},{9,8},{10,11... | collective-permute-start | bytes 589832 | tf_op jit(solution)/shard_map/ppermute | solution.py:470
  30.5 8.3 %collective-permute-start.12 = (bf16[128,768]{1,0:T(8,128)(2,1)S(1)}, bf16[128,768]{1,0:T(8,128)(2,1)S(1)}, u32[]{:S(2)}, u32[]{:S(2)}) collective-permute-start(bf16[128,768]{1,0:T(8,128)(2,1)S(1)} %project.4), channel_id=1, source_target_pairs={{0,1},{1,0},{2,3},{3,2},{4,5},{5,4},{6,7},{7,6},{8,9},{9,8},{10,11... | collective-permute-start | bytes 589832 | tf_op jit(solution)/shard_map/ppermute | solution.py:470

commit v2 on v0

--- a/solution.py
+++ b/solution.py
@@ -578,10 +578,13 @@
             flip=flip,
         )
 
+    got_side = call(
+        copy_kernel, shape((step, channels), bf16), [vmem], got_side, name="got", flops=20 * 10**9
+    )
+    for_far, got_side = lax.optimization_barrier((for_far, got_side))
+    got_far = flipped(for_far, "head", 2)
     for_side = [project(here, own_side, got_side, bf16, 0, 20 * 10**9)]
     from_side = [flipped(for_side[0], "head", 1)]
-    for_far, for_side[0] = lax.optimization_barrier((for_far, for_side[0]))
-    got_far = flipped(for_far, "head", 2)
     for_side.append(project(there, own_side, got_side, bf16, 1))
     from_side.append(flipped(for_side[1], "head", 1))
     state, for_side[1] = lax.optimization_barrier((state, for_side[1]))

time: 39.8 us -> 40.4 us (1.015)
  waiting for transfers between devices: 12.6 us -> 13.1 us
    ppermute x12, waiting for transfers between devices: 12.6 us -> 13.1 us  [flipped(): lax.ppermute(value, axis, [(i, i ^ flip) for i in range(lax.axis_size(axi...]
    pallas_call x14 -> x15, Pallas kernels: 7.87 us -> 7.9 us  [call(): pl.pallas_call(functools.partial(kernel, **keys_of) if keys_of else kerne...]
where the time goes in v2:
time: 40.4 us; the launch traced here: 40.2 us
  starting transfers between devices  17.4 us (43%)
  waiting for transfers between devices  13.1 us (32%)
  Pallas kernels  9.32 us (23%)
    ppermute x12, starting transfers between devices, flipped(): lax.ppermute(value, axis, [(i, i ^ flip) for i in range(lax.axis_size(axi...  14.8 us
    ppermute x12, waiting for transfers between devices, flipped(): lax.ppermute(value, axis, [(i, i ^ flip) for i in range(lax.axis_size(axi...  13.1 us
    pallas_call x15, Pallas kernels, call(): pl.pallas_call(functools.partial(kernel, **keys_of) if keys_of else kerne...  7.9 us
    pallas_call x2, Pallas kernels, two_by_two(): pl.pallas_call(functools.partial(add_kernel, flip=flip), out_shape=shape(...  1.42 us
    ppermute x1, starting transfers between devices, two_by_two(): first_tile = lax.ppermute(tile, 'tm', [(0, 1)])  1.34 us
    ppermute x1, starting transfers between devices, two_by_two(): first_edge = lax.ppermute(edge, 'tm', [(0, 1)])  1.32 us
  transfers between devices with their start and end apart: 14, of which 8 were waited for; matrix products, arithmetic and copies ran while one was open for 0% of the time, Pallas kernels for 19%

profile of v2, /device:TPU:0, one launch (start us, length us, event | category | flops | bytes accessed | tf_op | source)
XLA Modules:
  0.0 40.2 jit_solution(3941235655987003256)
XLA Ops:
  0.0 0.0 copy-start.2
  0.0 0.0 copy-start.3
  0.0 0.0 copy-start.1
  0.0 0.0 copy-start.5
  0.0 0.0 copy-start.4
  0.0 1.0 %part.1.part_ref = bf16[96,768]{1,0:T(8,128)(2,1)S(1)} custom-call(bf16[384,1536]{1,0:T(8,128)(2,1)} %w_ref.9), custom_call_target="tpu_custom_call" | custom-call | tf_op jit(solution)/shard_map/part/pallas_call | solution.py:458
  1.0 4.1 %collective-permute-start = (bf16[96,768]{1,0:T(8,128)(2,1)S(1)}, bf16[96,768]{1,0:T(8,128)(2,1)S(1)}, u32[]{:S(2)}, u32[]{:S(2)}) collective-permute-start(bf16[96,768]{1,0:T(8,128)(2,1)S(1)} %part.1.part_ref), channel_id=1, source_target_pairs={{0,2},{1,3},{2,0},{3,1},{4,6},{5,7},{6,4},{7,5},{8,10},{9,11},{10,... | collective-permute-start | bytes 442376 | tf_op jit(solution)/shard_map/ppermute | solution.py:470
  5.2 0.0 copy-done.2
  5.2 0.0 copy-done.3
  5.2 0.4 faces.1
  5.6 1.6 %collective-permute-start.1 = (bf16[2,2,64,384]{3,2,1,0:T(8,128)(2,1)S(1)}, bf16[2,2,64,384]{3,2,1,0:T(8,128)(2,1)S(1)}, u32[]{:S(2)}, u32[]{:S(2)}) collective-permute-start(bf16[2,2,64,384]{3,2,1,0:T(8,128)(2,1)S(1)} %get-tuple-element.65), channel_id=1, source_target_pairs={{0,8},{4,12},{8,0},{12,4},{1,9},{5,13},{9,1},{13,5},{2,10},{6,14},... | collective-permute-start | bytes 589832 | tf_op jit(solution)/shard_map/ppermute | solution.py:470
  7.1 1.5 %collective-permute-start.2 = (bf16[2,2,64,384]{3,2,1,0:T(8,128)(2,1)S(1)}, bf16[2,2,64,384]{3,2,1,0:T(8,128)(2,1)S(1)}, u32[]{:S(2)}, u32[]{:S(2)}) collective-permute-start(bf16[2,2,64,384]{3,2,1,0:T(8,128)(2,1)S(1)} %get-tuple-element.66), channel_id=1, source_target_pairs={{0,4},{4,0},{8,12},{12,8},{1,5},{5,1},{9,13},{13,9},{2,6},{6,2},{1... | collective-permute-start | bytes 589832 | tf_op jit(solution)/shard_map/ppermute | solution.py:470
  8.6 0.5 %collective-permute-start.3 = (bf16[2,2,16,384]{3,2,1,0:T(8,128)(2,1)S(1)}, bf16[2,2,16,384]{3,2,1,0:T(8,128)(2,1)S(1)}, u32[]{:S(2)}, u32[]{:S(2)}) collective-permute-start(bf16[2,2,16,384]{3,2,1,0:T(8,128)(2,1)S(1)} %get-tuple-element.67), channel_id=1, source_target_pairs={{0,12},{4,8},{8,4},{12,0},{1,13},{5,9},{9,5},{13,1},{2,14},{6,10},... | collective-permute-start | bytes 147464 | tf_op jit(solution)/shard_map/ppermute | solution.py:470
  9.1 0.0 copy-done.1
  9.1 0.0 copy-done.5
  9.1 0.0 copy-done.4
  9.1 1.4 %begin.1 = (f32[512,128]{1,0:T(8,128)S(1)}, f32[512,128]{1,0:T(8,128)S(1)}, f32[512,128]{1,0:T(8,128)S(1)}, s32[256,800]{1,0:T(8,128)S(1)}, s32[6,128]{1,0:T(8,128)S(1)}) custom-call(s32[3]{0:T(128)S(1)} %copy-done.5, s32[2,2,3]{2,1,0:T(2,128)S(1)} %bitcast.12, bf16[512,384]{1,0:T(8,128)(2,1)S(1)} %bitcast.5, bf16[2,512,384]{2,1,0:T(8,128)(2,1)S(1)} %get-tuple-element.55.tile_ref), custom_call_target="tpu_custom_call" | custom-call | tf_op jit(solution)/shard_map/begin/pallas_call | solution.py:458
  10.5 1.3 %collective-permute-start.7 = (bf16[2,512,384]{2,1,0:T(8,128)(2,1)S(1)}, bf16[2,512,384]{2,1,0:T(8,128)(2,1)S(1)}, u32[]{:S(2)}, u32[]{:S(2)}) collective-permute-start(bf16[2,512,384]{2,1,0:T(8,128)(2,1)S(1)} %get-tuple-element.55.tile_ref), channel_id=1, source_target_pairs={{0,16},{1,17},{2,18},{3,19},{4,20},{5,21},{6,22},{7,23},{8,24},{9,... | collective-permute-start | bytes 2359304 | tf_op jit(solution)/shard_map/ppermute | solution.py:517
  11.9 1.1 %tile.1 = (f32[512,256]{1,0:T(8,128)S(1)}, f32[512,256]{1,0:T(8,128)S(1)}, f32[512,256]{1,0:T(8,128)S(1)}) custom-call(bf16[512,384]{1,0:T(8,128)(2,1)S(1)} %bitcast.6, bf16[2,512,384]{2,1,0:T(8,128)(2,1)S(1)} %get-tuple-element.55.tile_ref, s32[256,800]{1,0:T(8,128)S(1)} %get-tuple-element.56.dist_ref.rest_3_, s32[6,128]{1,0:T(8,128)S(1)} %get-tuple-element.57.reach_ref.rest_4_), custom_call_target="tpu_custom_call" | custom-call | tf_op jit(solution)/shard_map/tile/pallas_call | solution.py:458
  12.9 0.0 collective-permute-done.in_ref
  13.0 1.3 %collective-permute-done.3.corner_ref = bf16[2,2,16,384]{3,2,1,0:T(8,128)(2,1)S(1)} collective-permute-done((bf16[2,2,16,384]{3,2,1,0:T(8,128)(2,1)S(1)}, bf16[2,2,16,384]{3,2,1,0:T(8,128)(2,1)S(1)}, u32[]{:S(2)}, u32[]{:S(2)}) %collective-permute-start.3) | collective-permute-done | bytes 49184 | tf_op jit(solution)/shard_map/ppermute | solution.py:470
  14.2 0.0 collective-permute-done.1.row_ref
  14.2 0.0 collective-permute-done.2.col_ref
  14.3 1.3 %collective-permute-start.8 = (bf16[2,288,384]{2,1,0:T(8,128)(2,1)S(1)}, bf16[2,288,384]{2,1,0:T(8,128)(2,1)S(1)}, u32[]{:S(2)}, u32[]{:S(2)}) collective-permute-start(bf16[2,288,384]{2,1,0:T(8,128)(2,1)S(1)} %edges.1.edge_ref), channel_id=1, source_target_pairs={{0,16},{1,17},{2,18},{3,19},{4,20},{5,21},{6,22},{7,23},{8,24},{9,... | collective-permute-start | bytes 1327112 | tf_op jit(solution)/shard_map/ppermute | solution.py:535
  15.6 1.6 %collective-permute-start.4 = (bf16[96,768]{1,0:T(8,128)(2,1)S(1)}, bf16[96,768]{1,0:T(8,128)(2,1)S(1)}, u32[]{:S(2)}, u32[]{:S(2)}) collective-permute-start(bf16[96,768]{1,0:T(8,128)(2,1)S(1)} %lone.1.refs_0_), channel_id=1, source_target_pairs={{0,4},{4,0},{8,12},{12,8},{1,5},{5,1},{9,13},{13,9},{2,6},{6,2},{1... | collective-permute-start | bytes 442376 | tf_op jit(solution)/shard_map/ppermute | solution.py:470
  17.2 1.5 %collective-permute-start.5 = (bf16[96,768]{1,0:T(8,128)(2,1)S(1)}, bf16[96,768]{1,0:T(8,128)(2,1)S(1)}, u32[]{:S(2)}, u32[]{:S(2)}) collective-permute-start(bf16[96,768]{1,0:T(8,128)(2,1)S(1)} %lone.1.refs_0_), channel_id=1, source_target_pairs={{0,8},{4,12},{8,0},{12,4},{1,9},{5,13},{9,1},{13,5},{2,10},{6,14},... | collective-permute-start | bytes 442376 | tf_op jit(solution)/shard_map/ppermute | solution.py:470
  18.7 0.5 %collective-permute-start.6 = (bf16[96,768]{1,0:T(8,128)(2,1)S(1)}, bf16[96,768]{1,0:T(8,128)(2,1)S(1)}, u32[]{:S(2)}, u32[]{:S(2)}) collective-permute-start(bf16[96,768]{1,0:T(8,128)(2,1)S(1)} %lone.1.refs_0_), channel_id=1, source_target_pairs={{0,12},{4,8},{8,4},{12,0},{1,13},{5,9},{9,5},{13,1},{2,14},{6,10},... | collective-permute-start | bytes 442376 | tf_op jit(solution)/shard_map/ppermute | solution.py:470
  19.2 0.0 collective-permute-done.8.first_edge_ref
  19.2 0.0 collective-permute-done.7.first_tile_ref
  19.2 0.7 %rest.3 = bf16[128,384]{1,0:T(8,128)(2,1)S(1)} custom-call(bf16[512,384]{1,0:T(8,128)(2,1)S(1)} %bitcast.7, bf16[2,288,384]{2,1,0:T(8,128)(2,1)S(1)} %edges.1.edge_ref, bf16[2,512,384]{2,1,0:T(8,128)(2,1)S(1)} %collective-permute-done.7.first_tile_ref, bf16[2,288,384]{2,1,0:T(8,128)(2,1)S(1)} %collective-permute-done.8.first_edge_ref, ...), custom_call_target="tpu_custom_call" | custom-call | tf_op jit(solution)/shard_map/rest/pallas_call | solution.py:458
  19.8 0.4 collective-permute-start.10
  20.2 1.2 %rest.4 = (bf16[128,384]{1,0:T(8,128)(2,1)S(1)}, bf16[128,384]{1,0:T(8,128)(2,1)S(1)}) custom-call(bf16[512,384]{1,0:T(8,128)(2,1)S(1)} %bitcast.8, bf16[2,288,384]{2,1,0:T(8,128)(2,1)S(1)} %edges.1.edge_ref, bf16[2,512,384]{2,1,0:T(8,128)(2,1)S(1)} %collective-permute-done.7.first_tile_ref, bf16[2,288,384]{2,1,0:T(8,128)(2,1)S(1)} %collective-permute-done.8.first_edge_ref, ...), custom_call_target="tpu_custom_call" | custom-call | tf_op jit(solution)/shard_map/rest/pallas_call | solution.py:458
  21.4 0.5 %collective-permute-done.4.refs_1_ = bf16[96,768]{1,0:T(8,128)(2,1)S(1)} collective-permute-done((bf16[96,768]{1,0:T(8,128)(2,1)S(1)}, bf16[96,768]{1,0:T(8,128)(2,1)S(1)}, u32[]{:S(2)}, u32[]{:S(2)}) %collective-permute-start.4) | collective-permute-done | bytes 147488 | tf_op jit(solution)/shard_map/ppermute | solution.py:470
  21.9 1.4 %collective-permute-done.5.refs_2_ = bf16[96,768]{1,0:T(8,128)(2,1)S(1)} collective-permute-done((bf16[96,768]{1,0:T(8,128)(2,1)S(1)}, bf16[96,768]{1,0:T(8,128)(2,1)S(1)}, u32[]{:S(2)}, u32[]{:S(2)}) %collective-permute-start.5) | collective-permute-done | bytes 147488 | tf_op jit(solution)/shard_map/ppermute | solution.py:470
  23.3 1.4 %collective-permute-done.6.refs_3_ = bf16[96,768]{1,0:T(8,128)(2,1)S(1)} collective-permute-done((bf16[96,768]{1,0:T(8,128)(2,1)S(1)}, bf16[96,768]{1,0:T(8,128)(2,1)S(1)}, u32[]{:S(2)}, u32[]{:S(2)}) %collective-permute-start.6) | collective-permute-done | bytes 147488 | tf_op jit(solution)/shard_map/ppermute | solution.py:470
  24.7 0.1 stack.1.part_ref
  24.8 0.0 copy-start
  24.8 0.1 collective-permute-start.9
  24.9 0.5 %collective-permute-done.10.in_ref = bf16[128,384]{1,0:T(8,128)(2,1)S(1)} collective-permute-done((bf16[128,384]{1,0:T(8,128)(2,1)S(1)}, bf16[128,384]{1,0:T(8,128)(2,1)S(1)}, u32[]{:S(2)}, u32[]{:S(2)}) %collective-permute-start.10) | collective-permute-done | bytes 98336 | tf_op jit(solution)/shard_map/ppermute | solution.py:470
  25.4 0.5 %collective-permute-start.11 = (bf16[128,384]{1,0:T(8,128)(2,1)S(1)}, bf16[128,384]{1,0:T(8,128)(2,1)S(1)}, u32[]{:S(2)}, u32[]{:S(2)}) collective-permute-start(bf16[128,384]{1,0:T(8,128)(2,1)S(1)} %get-tuple-element.92), channel_id=1, source_target_pairs={{0,2},{1,3},{2,0},{3,1},{4,6},{5,7},{6,4},{7,5},{8,10},{9,11},{10,... | collective-permute-start | bytes 294920 | tf_op jit(solution)/shard_map/ppermute | solution.py:470
  25.9 0.1 copy-done
  26.1 0.4 project.7
  26.4 2.5 %collective-permute-start.13 = (bf16[128,768]{1,0:T(8,128)(2,1)S(1)}, bf16[128,768]{1,0:T(8,128)(2,1)S(1)}, u32[]{:S(2)}, u32[]{:S(2)}) collective-permute-start(bf16[128,768]{1,0:T(8,128)(2,1)S(1)} %project.7), channel_id=1, source_target_pairs={{0,1},{1,0},{2,3},{3,2},{4,5},{5,4},{6,7},{7,6},{8,9},{9,8},{10,11... | collective-permute-start | bytes 589832 | tf_op jit(solution)/shard_map/ppermute | solution.py:470
  28.9 0.0 collective-permute-done.9.part_ref
  28.9 0.4 project.4
  29.3 0.1 collective-permute-start.12
  29.4 0.7 %rest.5.own_ref = bf16[128,384]{1,0:T(8,128)(2,1)S(1)} custom-call(bf16[512,384]{1,0:T(8,128)(2,1)S(1)} %bitcast.9, bf16[2,288,384]{2,1,0:T(8,128)(2,1)S(1)} %edges.1.edge_ref, bf16[2,512,384]{2,1,0:T(8,128)(2,1)S(1)} %collective-permute-done.7.first_tile_ref, bf16[2,288,384]{2,1,0:T(8,128)(2,1)S(1)} %collective-permute-done.8.first_edge_ref, ...), custom_call_target="tpu_custom_call" | custom-call | flops 20000000000 | tf_op jit(solution)/shard_map/rest/pallas_call | solution.py:458
  30.1 3.2 %collective-permute-done.11.got_ref = bf16[128,384]{1,0:T(8,128)(2,1)S(1)} collective-permute-done((bf16[128,384]{1,0:T(8,128)(2,1)S(1)}, bf16[128,384]{1,0:T(8,128)(2,1)S(1)}, u32[]{:S(2)}, u32[]{:S(2)}) %collective-permute-start.11) | collective-permute-done | bytes 98336 | tf_op jit(solution)/shard_map/ppermute | solution.py:470
  33.3 0.4 project.5.mine_ref
  33.6 0.4 project.6.mine_ref
  34.0 1.6 %collective-permute-done.13.got_ref = bf16[128,768]{1,0:T(8,128)(2,1)S(1)} collective-permute-done((bf16[128,768]{1,0:T(8,128)(2,1)S(1)}, bf16[128,768]{1,0:T(8,128)(2,1)S(1)}, u32[]{:S(2)}, u32[]{:S(2)}) %collective-permute-start.13) | collective-permute-done | bytes 196640 | tf_op jit(solution)/shard_map/ppermute | solution.py:470
  35.6 0.7 %add.2.rest_0_ = bf16[128,1536]{1,0:T(8,128)(2,1)} custom-call(f32[128,768]{1,0:T(8,128)S(1)} %project.6.mine_ref, bf16[128,768]{1,0:T(8,128)(2,1)S(1)} %collective-permute-done.13.got_ref), custom_call_target="tpu_custom_call" | custom-call | tf_op jit(solution)/shard_map/add/pallas_call | solution.py:600
  36.4 3.1 %collective-permute-done.12.got_ref = bf16[128,768]{1,0:T(8,128)(2,1)S(1)} collective-permute-done((bf16[128,768]{1,0:T(8,128)(2,1)S(1)}, bf16[128,768]{1,0:T(8,128)(2,1)S(1)}, u32[]{:S(2)}, u32[]{:S(2)}) %collective-permute-start.12) | collective-permute-done | bytes 196640 | tf_op jit(solution)/shard_map/ppermute | solution.py:470
  39.5 0.7 %add.3 = bf16[128,1536]{1,0:T(8,128)(2,1)} custom-call(f32[128,768]{1,0:T(8,128)S(1)} %project.5.mine_ref, bf16[128,768]{1,0:T(8,128)(2,1)S(1)} %collective-permute-done.12.got_ref, bf16[128,1536]{1,0:T(8,128)(2,1)} %add.2.rest_0_), custom_call_target="tpu_custom_call", output_to_operand_aliasing={{}: (2, {})} | custom-call | tf_op jit(solution)/shard_map/add/pallas_call | solution.py:600
  (3 shorter events, 0.1 us)
Async XLA Ops:
  0.0 5.2 %copy-start.2 = (bf16[1,1,2,16,16,384]{5,4,3,2,1,0:T(8,128)(2,1)S(1)}, bf16[1,1,2,16,16,384]{5,4,3,2,1,0:T(8,128)(2,1)}, u32[]{:S(2)}) copy-start(bf16[1,1,2,16,16,384]{5,4,3,2,1,0:T(8,128)(2,1)} %param.7) | copy-start | bytes 1179652
  0.0 5.2 %copy-start.3 = (bf16[1,1,2,16,16,384]{5,4,3,2,1,0:T(8,128)(2,1)S(1)}, bf16[1,1,2,16,16,384]{5,4,3,2,1,0:T(8,128)(2,1)}, u32[]{:S(2)}) copy-start(bf16[1,1,2,16,16,384]{5,4,3,2,1,0:T(8,128)(2,1)} %param.8) | copy-start | bytes 1179652
  0.0 9.1 %copy-start.1 = (bf16[1,1,2,16,16,384]{5,4,3,2,1,0:T(8,128)(2,1)S(1)}, bf16[1,1,2,16,16,384]{5,4,3,2,1,0:T(8,128)(2,1)}, u32[]{:S(2)}) copy-start(bf16[1,1,2,16,16,384]{5,4,3,2,1,0:T(8,128)(2,1)} %param.6) | copy-start | bytes 1179652
  0.0 9.1 %copy-start.5 = (s32[3]{0:T(128)S(1)}, s32[3]{0:T(128)}, u32[]{:S(2)}) copy-start(s32[3]{0:T(128)} %radius_ref.1) | copy-start | bytes 40
  0.0 9.1 %copy-start.4 = (s32[3,2,2]{0,2,1:T(2,128)S(1)}, s32[3,2,2]{0,2,1:T(2,128)}, u32[]{:S(2)}) copy-start(s32[3,2,2]{0,2,1:T(2,128)} %param.11) | copy-start | bytes 148
  1.0 11.9 %collective-permute-start = (bf16[96,768]{1,0:T(8,128)(2,1)S(1)}, bf16[96,768]{1,0:T(8,128)(2,1)S(1)}, u32[]{:S(2)}, u32[]{:S(2)}) collective-permute-start(bf16[96,768]{1,0:T(8,128)(2,1)S(1)} %part.1.part_ref), channel_id=1, source_target_pairs={{0,2},{1,3},{2,0},{3,1},{4,6},{5,7},{6,4},{7,5},{8,10},{9,11},{10,... | collective-permute-start | bytes 442376 | tf_op jit(solution)/shard_map/ppermute | solution.py:470
  5.6 8.7 %collective-permute-start.1 = (bf16[2,2,64,384]{3,2,1,0:T(8,128)(2,1)S(1)}, bf16[2,2,64,384]{3,2,1,0:T(8,128)(2,1)S(1)}, u32[]{:S(2)}, u32[]{:S(2)}) collective-permute-start(bf16[2,2,64,384]{3,2,1,0:T(8,128)(2,1)S(1)} %get-tuple-element.65), channel_id=1, source_target_pairs={{0,8},{4,12},{8,0},{12,4},{1,9},{5,13},{9,1},{13,5},{2,10},{6,14},... | collective-permute-start | bytes 589832 | tf_op jit(solution)/shard_map/ppermute | solution.py:470
  7.1 7.1 %collective-permute-start.2 = (bf16[2,2,64,384]{3,2,1,0:T(8,128)(2,1)S(1)}, bf16[2,2,64,384]{3,2,1,0:T(8,128)(2,1)S(1)}, u32[]{:S(2)}, u32[]{:S(2)}) collective-permute-start(bf16[2,2,64,384]{3,2,1,0:T(8,128)(2,1)S(1)} %get-tuple-element.66), channel_id=1, source_target_pairs={{0,4},{4,0},{8,12},{12,8},{1,5},{5,1},{9,13},{13,9},{2,6},{6,2},{1... | collective-permute-start | bytes 589832 | tf_op jit(solution)/shard_map/ppermute | solution.py:470
  8.6 5.6 %collective-permute-start.3 = (bf16[2,2,16,384]{3,2,1,0:T(8,128)(2,1)S(1)}, bf16[2,2,16,384]{3,2,1,0:T(8,128)(2,1)S(1)}, u32[]{:S(2)}, u32[]{:S(2)}) collective-permute-start(bf16[2,2,16,384]{3,2,1,0:T(8,128)(2,1)S(1)} %get-tuple-element.67), channel_id=1, source_target_pairs={{0,12},{4,8},{8,4},{12,0},{1,13},{5,9},{9,5},{13,1},{2,14},{6,10},... | collective-permute-start | bytes 147464 | tf_op jit(solution)/shard_map/ppermute | solution.py:470
  10.5 8.7 %collective-permute-start.7 = (bf16[2,512,384]{2,1,0:T(8,128)(2,1)S(1)}, bf16[2,512,384]{2,1,0:T(8,128)(2,1)S(1)}, u32[]{:S(2)}, u32[]{:S(2)}) collective-permute-start(bf16[2,512,384]{2,1,0:T(8,128)(2,1)S(1)} %get-tuple-element.55.tile_ref), channel_id=1, source_target_pairs={{0,16},{1,17},{2,18},{3,19},{4,20},{5,21},{6,22},{7,23},{8,24},{9,... | collective-permute-start | bytes 2359304 | tf_op jit(solution)/shard_map/ppermute | solution.py:517
  14.3 4.9 %collective-permute-start.8 = (bf16[2,288,384]{2,1,0:T(8,128)(2,1)S(1)}, bf16[2,288,384]{2,1,0:T(8,128)(2,1)S(1)}, u32[]{:S(2)}, u32[]{:S(2)}) collective-permute-start(bf16[2,288,384]{2,1,0:T(8,128)(2,1)S(1)} %edges.1.edge_ref), channel_id=1, source_target_pairs={{0,16},{1,17},{2,18},{3,19},{4,20},{5,21},{6,22},{7,23},{8,24},{9,... | collective-permute-start | bytes 1327112 | tf_op jit(solution)/shard_map/ppermute | solution.py:535
  15.6 6.3 %collective-permute-start.4 = (bf16[96,768]{1,0:T(8,128)(2,1)S(1)}, bf16[96,768]{1,0:T(8,128)(2,1)S(1)}, u32[]{:S(2)}, u32[]{:S(2)}) collective-permute-start(bf16[96,768]{1,0:T(8,128)(2,1)S(1)} %lone.1.refs_0_), channel_id=1, source_target_pairs={{0,4},{4,0},{8,12},{12,8},{1,5},{5,1},{9,13},{13,9},{2,6},{6,2},{1... | collective-permute-start | bytes 442376 | tf_op jit(solution)/shard_map/ppermute | solution.py:470
  17.2 6.1 %collective-permute-start.5 = (bf16[96,768]{1,0:T(8,128)(2,1)S(1)}, bf16[96,768]{1,0:T(8,128)(2,1)S(1)}, u32[]{:S(2)}, u32[]{:S(2)}) collective-permute-start(bf16[96,768]{1,0:T(8,128)(2,1)S(1)} %lone.1.refs_0_), channel_id=1, source_target_pairs={{0,8},{4,12},{8,0},{12,4},{1,9},{5,13},{9,1},{13,5},{2,10},{6,14},... | collective-permute-start | bytes 442376 | tf_op jit(solution)/shard_map/ppermute | solution.py:470
  18.7 6.1 %collective-permute-start.6 = (bf16[96,768]{1,0:T(8,128)(2,1)S(1)}, bf16[96,768]{1,0:T(8,128)(2,1)S(1)}, u32[]{:S(2)}, u32[]{:S(2)}) collective-permute-start(bf16[96,768]{1,0:T(8,128)(2,1)S(1)} %lone.1.refs_0_), channel_id=1, source_target_pairs={{0,12},{4,8},{8,4},{12,0},{1,13},{5,9},{9,5},{13,1},{2,14},{6,10},... | collective-permute-start | bytes 442376 | tf_op jit(solution)/shard_map/ppermute | solution.py:470
  19.8 5.6 %collective-permute-start.10 = (bf16[128,384]{1,0:T(8,128)(2,1)S(1)}, bf16[128,384]{1,0:T(8,128)(2,1)S(1)}, u32[]{:S(2)}, u32[]{:S(2)}) collective-permute-start(bf16[128,384]{1,0:T(8,128)(2,1)S(1)} %rest.3), channel_id=1, source_target_pairs={{0,2},{1,3},{2,0},{3,1},{4,6},{5,7},{6,4},{7,5},{8,10},{9,11},{10,... | collective-permute-start | bytes 294920 | tf_op jit(solution)/shard_map/ppermute | solution.py:470
  24.8 1.3 %copy-start = (bf16[384,1536]{1,0:T(8,128)(2,1)S(1)}, bf16[384,1536]{1,0:T(8,128)(2,1)}, u32[]{:S(2)}) copy-start(bf16[384,1536]{1,0:T(8,128)(2,1)} %w_ref.9) | copy-start | bytes 3538948
  24.8 4.1 %collective-permute-start.9 = (bf16[384,768]{1,0:T(8,128)(2,1)S(1)}, bf16[384,768]{1,0:T(8,128)(2,1)S(1)}, u32[]{:S(2)}, u32[]{:S(2)}) collective-permute-start(bf16[384,768]{1,0:T(8,128)(2,1)S(1)} %stack.1.part_ref), channel_id=1, source_target_pairs={{0,16},{16,0},{1,17},{17,1},{2,18},{18,2},{3,19},{19,3},{4,20},{20... | collective-permute-start | bytes 1769480 | tf_op jit(solution)/shard_map/ppermute | solution.py:470
  25.4 7.8 %collective-permute-start.11 = (bf16[128,384]{1,0:T(8,128)(2,1)S(1)}, bf16[128,384]{1,0:T(8,128)(2,1)S(1)}, u32[]{:S(2)}, u32[]{:S(2)}) collective-permute-start(bf16[128,384]{1,0:T(8,128)(2,1)S(1)} %get-tuple-element.92), channel_id=1, source_target_pairs={{0,2},{1,3},{2,0},{3,1},{4,6},{5,7},{6,4},{7,5},{8,10},{9,11},{10,... | collective-permute-start | bytes 294920 | tf_op jit(solution)/shard_map/ppermute | solution.py:470
  26.4 9.2 %collective-permute-start.13 = (bf16[128,768]{1,0:T(8,128)(2,1)S(1)}, bf16[128,768]{1,0:T(8,128)(2,1)S(1)}, u32[]{:S(2)}, u32[]{:S(2)}) collective-permute-start(bf16[128,768]{1,0:T(8,128)(2,1)S(1)} %project.7), channel_id=1, source_target_pairs={{0,1},{1,0},{2,3},{3,2},{4,5},{5,4},{6,7},{7,6},{8,9},{9,8},{10,11... | collective-permute-start | bytes 589832 | tf_op jit(solution)/shard_map/ppermute | solution.py:470
  29.3 10.2 %collective-permute-start.12 = (bf16[128,768]{1,0:T(8,128)(2,1)S(1)}, bf16[128,768]{1,0:T(8,128)(2,1)S(1)}, u32[]{:S(2)}, u32[]{:S(2)}) collective-permute-start(bf16[128,768]{1,0:T(8,128)(2,1)S(1)} %project.4), channel_id=1, source_target_pairs={{0,1},{1,0},{2,3},{3,2},{4,5},{5,4},{6,7},{7,6},{8,9},{9,8},{10,11... | collective-permute-start | bytes 589832 | tf_op jit(solution)/shard_map/ppermute | solution.py:470
